TPU v7x, 32 devices: a whole 2x2x4 slice. The times are simulated.
32 devices in a mesh: freq: 2 (over x), geo: 16 (over z, y, core).
Axes of the slice: x: 2, y: 2, z: 4, core: 2. Of those that a mesh axis runs over, the one named last changes fastest.
Arguments:
- energy: float32 [64, 48, 36, 128], P('geo', 'freq'), may hold values from 0.1 to 1.5
- water_depth: float32 [64, 128], P('geo'), may hold values from 0.5 to 4
- wet_mask: int32 [64, 128], P('geo'), may hold values 0 or 1
- vegetation: int32 [64, 128], P('geo'), may hold values 0 or 1
- canopy: float32 [64, 128], P('geo'), may hold values from 0.004 to 0.04
- quad_offsets: int32 [4], replicated, may hold values from 1 to 3, as said below
- quad_weights: float32 [2], replicated, may hold values from 0.2 to 0.8
Outputs:
- energy_next: float32 [64, 48, 36, 128], P('geo', 'freq')
- orbital: float32 [64, 128], P('geo')
Inputs may be any that keep to these rules, and one draw needn't show every extreme that they name: `quad_offsets`: offsets a and the two direction turns lie in 1 .. 3; the lower frequency offset b equals 3 in every draw.
All inputs are finite; a program needn't handle non-finite values. No bound on the sum of `wet_mask` or of `vegetation` on one device may be relied on, other than what follows from the above.
Results may differ from a plain program's by a relative error of at most 0.00002.
Values sent between devices are 32-bit elements; how exact they have to be, the bound alone decides.
A program may use at most 64 MiB of HBM per device.

v0:
```python
import math

import jax
import jax.numpy as jnp
from jax import lax
from jax.sharding import PartitionSpec as P

FH = 4
SUBSTEPS = 8


gravity = 9.81
base_freq = 0.03
freq_ratio = 1.05
cell_size = 20.0
sub_step = 2.0
coupling = 0.01
coef_plus = 0.4096
coef_minus = 3.1605
coef_both = 2.589


def padded(block, sides, width):
    for axis, dim in sides:
        count = lax.axis_size(axis)
        forward = [(i, i + 1) for i in range(count - 1)]
        backward = [(target, source) for source, target in forward]
        low = lax.ppermute(
            lax.slice_in_dim(block, block.shape[dim] - width, None, axis=dim), axis, forward
        )
        high = lax.ppermute(lax.slice_in_dim(block, 0, width, axis=dim), axis, backward)
        block = jnp.concatenate([low, block, high], axis=dim)
    return block


def physics(radian_freq, water_depth, dir_count):
    square = (radian_freq * radian_freq)[None, :, None]
    column = water_depth[:, None, :]
    depth_ratio = square * column / gravity
    depth_wave = depth_ratio / jnp.sqrt(jnp.tanh(depth_ratio))
    group_speed = (
        radian_freq[None, :, None]
        * column
        / depth_wave
        * (0.5 + depth_wave / jnp.sinh(2.0 * depth_wave))
    )
    orbit_weight = (
        square
        / jnp.sinh(depth_wave) ** 2
        * (radian_freq * (freq_ratio - 1.0))[None, :, None]
        * (2.0 * math.pi / dir_count)
    )
    return (group_speed, orbit_weight)


def angles_of(dir_count):
    angles = (jnp.arange(dir_count, dtype=jnp.float32) + 0.5) * (2.0 * math.pi / dir_count)
    return (jnp.cos(angles), jnp.sin(angles))


def shifted(doubled, freq_off, dir_off, count):
    dir_count = doubled.shape[2] // 2
    starts = (
        jnp.zeros((), jnp.int32),
        freq_off + FH,
        dir_off % dir_count,
        jnp.zeros((), jnp.int32),
    )
    return lax.dynamic_slice(
        doubled, starts, (doubled.shape[0], count, dir_count, doubled.shape[3])
    )


def interaction(extended, masked, quad_offsets, quad_weights):
    count = masked.shape[1]
    doubled = jnp.concatenate([extended, extended], axis=2)
    up_bins, down_bins, up_turn, down_turn = (
        quad_offsets[0],
        quad_offsets[1],
        quad_offsets[2],
        quad_offsets[3],
    )
    weight_up, weight_down = (quad_weights[0], quad_weights[1])
    upper = weight_up * shifted(doubled, up_bins, up_turn, count) + (1.0 - weight_up) * shifted(
        doubled, up_bins + 1, up_turn, count
    )
    lower = weight_down * shifted(doubled, -down_bins, -down_turn, count) + (
        1.0 - weight_down
    ) * shifted(doubled, -down_bins - 1, -down_turn, count)
    return coupling * (
        masked * masked * (coef_plus * upper + coef_minus * lower)
        - coef_both * masked * upper * lower
    )


def redistribute(extended, transfer, quad_offsets, quad_weights):
    count = transfer.shape[1]
    doubled = jnp.concatenate([extended, extended], axis=2)
    up_bins, down_bins, up_turn, down_turn = (
        quad_offsets[0],
        quad_offsets[1],
        quad_offsets[2],
        quad_offsets[3],
    )
    weight_up, weight_down = (quad_weights[0], quad_weights[1])
    gained = weight_up * shifted(doubled, -up_bins, -up_turn, count) + (1.0 - weight_up) * shifted(
        doubled, -up_bins - 1, -up_turn, count
    )
    gained = (
        gained
        + weight_down * shifted(doubled, down_bins, down_turn, count)
        + (1.0 - weight_down) * shifted(doubled, down_bins + 1, down_turn, count)
    )
    return gained - 2.0 * transfer


def east_west(east_flux, cosines):
    zeros = jnp.zeros_like(east_flux[..., :1])
    behind = jnp.concatenate([zeros, east_flux[..., :-1]], axis=-1)
    ahead = jnp.concatenate([east_flux[..., 1:], zeros], axis=-1)
    east_going = (cosines > 0.0).astype(jnp.float32)[None, None, :, None]
    return east_going * (east_flux - behind) + (1.0 - east_going) * (ahead - east_flux)


def body(energy, water_depth, wet_mask, vegetation, canopy, quad_offsets, quad_weights):
    tile_rows, freq_count, dir_count, tile_cols = energy.shape
    wet_field = wet_mask.astype(jnp.float32)
    veg_field = vegetation.astype(jnp.float32)
    wet_four = wet_field[:, None, None, :]
    masked = wet_four * energy
    first_bin = lax.axis_index("freq") * freq_count
    bin_index = (first_bin + jnp.arange(freq_count, dtype=jnp.int32)).astype(jnp.float32)
    radian_freq = 2.0 * math.pi * base_freq * jnp.power(freq_ratio, bin_index)
    group_speed, orbit_weight = physics(radian_freq, water_depth, dir_count)
    partial_value = jnp.sum(orbit_weight * jnp.sum(energy, axis=2), axis=1)
    orbital = jnp.sqrt(lax.psum(partial_value, "freq"))
    full_step = SUBSTEPS * sub_step
    damping = 1.0 + full_step * canopy * veg_field * orbital
    extended = padded(masked, (("freq", 1),), FH)
    transfer = interaction(extended, masked, quad_offsets, quad_weights)
    spread = padded(transfer, (("freq", 1),), FH)
    change = redistribute(spread, transfer, quad_offsets, quad_weights)
    increment = (masked + full_step * change) / damping[:, None, None, :] - masked
    cosines, sines = angles_of(dir_count)
    step_ratio = sub_step / cell_size
    east_speed = group_speed[:, :, None, :] * cosines[None, None, :, None]
    north_speed = group_speed[:, :, None, :] * sines[None, None, :, None]
    north_going = (sines > 0.0).astype(jnp.float32)[None, None, :, None]
    spectrum = masked
    for substep in range(SUBSTEPS):
        east_flux = east_speed * spectrum
        north_flux = north_speed * spectrum
        rimmed = padded(north_flux, (("geo", 0),), 1)
        below = rimmed[:-2]
        above = rimmed[2:]
        along = north_going * (north_flux - below) + (1.0 - north_going) * (above - north_flux)
        spectrum = wet_four * (spectrum - step_ratio * (east_west(east_flux, cosines) + along))
    return (wet_four * (spectrum + increment), orbital)


def solution(mesh):
    placed = (
        P("geo", "freq", None, None),
        P("geo", None),
        P("geo", None),
        P("geo", None),
        P("geo", None),
        P(),
        P(),
    )
    return jax.shard_map(
        body,
        mesh=mesh,
        in_specs=placed,
        out_specs=(P("geo", "freq", None, None), P("geo", None)),
        check_vma=False,
    )
```

profile of v0, /device:TPU:17, one launch (start us, length us, event | category | flops | bytes accessed | tf_op | source)
XLA Modules:
  0.0 174.3 jit_solution(7239628528747887890)
XLA Ops:
  5.9 4.0 %collective-permute-start.16 = (f32[4,4,36,128]{3,2,1,0:T(8,128)S(1)}, f32[4,4,36,128]{3,2,1,0:T(8,128)S(1)}, u32[]{:S(2)}, u32[]{:S(2)}) collective-permute-start(f32[4,4,36,128]{3,2,1,0:T(8,128)S(1)} %get-tuple-element.26), channel_id=1, source_target_pairs={{0,16},{1,17},{2,18},{3,19},{4,20},{5,21},{6,22},{7,23},{8,24},{9,... | collective-permute-start | bytes 884744 | tf_op jit(solution)/shard_map/ppermute | solution.py:28
  17.6 2.6 %maximum_maximum_fusion = f32[4,32,72,128]{3,2,1,0:T(8,128)S(1)} fusion(f32[4,4,36,128]{3,2,1,0:T(8,128)S(1)} %collective-permute-done.17, f32[4,24,36,128]{3,2,1,0:T(8,128)} %copy-done.10, f32[4,4,36,128]{3,2,1,0:T(8,128)S(1)} %collective-permute-done.16), kind=kLoop, calls=%fused_computation.16 | loop fusion | flops 5898240 | bytes 7077888 | tf_op jit(solution)/shard_map/concatenate | solution.py:76
  20.2 5.3 %broadcast_multiply_fusion = (f32[4,24,36,128]{3,2,1,0:T(8,128)}, f32[4,24,36,128]{3,2,1,0:T(8,128)}, f32[4,24,36,128]{3,2,1,0:T(8,128)S(1)}, f32[4,24,36,128]{3,2,1,0:T(8,128)S(1)}) fusion(f32[4,32,72,128]{3,2,1,0:T(8,128)S(1)} %maximum_maximum_fusion, s32[]{:T(128)S(6)} %select_n.74, s32[]{:T(128)S(6)} %select_n.73, f32[]{:T(128)S(6)} %sub.240, ...), kind=kLoop, calls=%fused_computation.110 | loop fusion | flops 9289728 | bytes 15976776 | tf_op jit(solution)/shard_map/mul | solution.py:90
  25.7 3.1 %collective-permute-start.1 = (f32[1,24,36,128]{3,2,1,0:T(8,128)S(1)}, f32[1,24,36,128]{3,2,1,0:T(8,128)S(1)}, u32[]{:S(2)}, u32[]{:S(2)}) collective-permute-start(f32[1,24,36,128]{3,2,1,0:T(8,128)S(1)} %get-tuple-element.57), channel_id=1, source_target_pairs={{1,0},{2,1},{3,2},{4,3},{5,4},{6,5},{7,6},{8,7},{9,8},{10,9},{11,1... | collective-permute-start | bytes 1327112 | tf_op jit(solution)/shard_map/ppermute | solution.py:31
  28.8 3.0 %collective-permute-start = (f32[1,24,36,128]{3,2,1,0:T(8,128)S(1)}, f32[1,24,36,128]{3,2,1,0:T(8,128)S(1)}, u32[]{:S(2)}, u32[]{:S(2)}) collective-permute-start(f32[1,24,36,128]{3,2,1,0:T(8,128)S(1)} %get-tuple-element.56), channel_id=1, source_target_pairs={{0,1},{1,2},{2,3},{3,4},{4,5},{5,6},{6,7},{7,8},{8,9},{9,10},{10,1... | collective-permute-start | bytes 1327112 | tf_op jit(solution)/shard_map/ppermute | solution.py:28
  32.6 9.2 %collective-permute-done.1 = f32[1,24,36,128]{3,2,1,0:T(8,128)S(1)} collective-permute-done((f32[1,24,36,128]{3,2,1,0:T(8,128)S(1)}, f32[1,24,36,128]{3,2,1,0:T(8,128)S(1)}, u32[]{:S(2)}, u32[]{:S(2)}) %collective-permute-start.1) | collective-permute-done | bytes 442400 | tf_op jit(solution)/shard_map/ppermute | solution.py:31
  45.9 4.0 %collective-permute-start.2 = (f32[1,24,36,128]{3,2,1,0:T(8,128)S(1)}, f32[1,24,36,128]{3,2,1,0:T(8,128)S(1)}, u32[]{:S(2)}, u32[]{:S(2)}) collective-permute-start(f32[1,24,36,128]{3,2,1,0:T(8,128)S(1)} %get-tuple-element.52), channel_id=1, source_target_pairs={{0,1},{1,2},{2,3},{3,4},{4,5},{5,6},{6,7},{7,8},{8,9},{9,10},{10,1... | collective-permute-start | bytes 1327112 | tf_op jit(solution)/shard_map/ppermute | solution.py:28
  50.5 9.2 %collective-permute-done.3 = f32[1,24,36,128]{3,2,1,0:T(8,128)S(1)} collective-permute-done((f32[1,24,36,128]{3,2,1,0:T(8,128)S(1)}, f32[1,24,36,128]{3,2,1,0:T(8,128)S(1)}, u32[]{:S(2)}, u32[]{:S(2)}) %collective-permute-start.3) | collective-permute-done | bytes 442400 | tf_op jit(solution)/shard_map/ppermute | solution.py:31
  63.6 3.6 %collective-permute-start.4 = (f32[1,24,36,128]{3,2,1,0:T(8,128)S(1)}, f32[1,24,36,128]{3,2,1,0:T(8,128)S(1)}, u32[]{:S(2)}, u32[]{:S(2)}) collective-permute-start(f32[1,24,36,128]{3,2,1,0:T(8,128)S(1)} %get-tuple-element.48), channel_id=1, source_target_pairs={{0,1},{1,2},{2,3},{3,4},{4,5},{5,6},{6,7},{7,8},{8,9},{9,10},{10,1... | collective-permute-start | bytes 1327112 | tf_op jit(solution)/shard_map/ppermute | solution.py:28
  67.9 8.9 %collective-permute-done.5 = f32[1,24,36,128]{3,2,1,0:T(8,128)S(1)} collective-permute-done((f32[1,24,36,128]{3,2,1,0:T(8,128)S(1)}, f32[1,24,36,128]{3,2,1,0:T(8,128)S(1)}, u32[]{:S(2)}, u32[]{:S(2)}) %collective-permute-start.5) | collective-permute-done | bytes 442400 | tf_op jit(solution)/shard_map/ppermute | solution.py:31
  80.6 3.6 %collective-permute-start.6 = (f32[1,24,36,128]{3,2,1,0:T(8,128)S(1)}, f32[1,24,36,128]{3,2,1,0:T(8,128)S(1)}, u32[]{:S(2)}, u32[]{:S(2)}) collective-permute-start(f32[1,24,36,128]{3,2,1,0:T(8,128)S(1)} %get-tuple-element.44), channel_id=1, source_target_pairs={{0,1},{1,2},{2,3},{3,4},{4,5},{5,6},{6,7},{7,8},{8,9},{9,10},{10,1... | collective-permute-start | bytes 1327112 | tf_op jit(solution)/shard_map/ppermute | solution.py:28
  84.9 8.5 %collective-permute-done.7 = f32[1,24,36,128]{3,2,1,0:T(8,128)S(1)} collective-permute-done((f32[1,24,36,128]{3,2,1,0:T(8,128)S(1)}, f32[1,24,36,128]{3,2,1,0:T(8,128)S(1)}, u32[]{:S(2)}, u32[]{:S(2)}) %collective-permute-start.7) | collective-permute-done | bytes 442400 | tf_op jit(solution)/shard_map/ppermute | solution.py:31
  100.7 3.6 %collective-permute-start.8 = (f32[1,24,36,128]{3,2,1,0:T(8,128)S(1)}, f32[1,24,36,128]{3,2,1,0:T(8,128)S(1)}, u32[]{:S(2)}, u32[]{:S(2)}) collective-permute-start(f32[1,24,36,128]{3,2,1,0:T(8,128)S(1)} %get-tuple-element.40), channel_id=1, source_target_pairs={{0,1},{1,2},{2,3},{3,4},{4,5},{5,6},{6,7},{7,8},{8,9},{9,10},{10,1... | collective-permute-start | bytes 1327112 | tf_op jit(solution)/shard_map/ppermute | solution.py:28
  104.3 4.0 %psum.7 = f32[4,128]{1,0:T(4,128)S(1)} all-reduce(f32[4,128]{1,0:T(4,128)S(1)} %get-tuple-element.62), channel_id=1, replica_groups=mesh['freq'=2,'geo'=16] {'freq'}, use_global_device_ids=true, to_apply=%region_2.0 | all-reduce | flops 512 | bytes 4096 | tf_op jit(solution)/shard_map/psum | solution.py:136
  108.3 2.9 %fusion.102 = (f32[4,24,36,127]{3,2,1,0:T(8,128)S(1)}, f32[4,24,36,127]{3,2,1,0:T(8,128)S(1)}) fusion(f32[4,24,36,128]{3,2,1,0:T(8,128)} %get-tuple-element.14), kind=kLoop, calls=%fused_computation.147 | loop fusion | bytes 7022592 | tf_op jit(solution)/shard_map/slice | solution.py:119
  113.1 2.5 %multiply_multiply_fusion.10 = (f32[4,24,36,128]{3,2,1,0:T(8,128)}, f32[4,24,36,128]{3,2,1,0:T(8,128)S(1)}) fusion(f32[36]{0:T(128)S(1)} %fusion.83, f32[4,24,128]{2,1,0:T(8,128)S(1)} %get-tuple-element.63, f32[4,24,36,128]{3,2,1,0:T(8,128)S(1)} %copy-done.4, f32[4,24,36,128]{3,2,1,0:T(8,128)S(1)} %copy-done.8, ...), kind=kLoop, calls=%fused_computation.10 | loop fusion | flops 8404992 | bytes 11525840 | tf_op jit(solution)/shard_map/mul | solution.py:151
  120.4 3.6 %collective-permute-start.10 = (f32[1,24,36,128]{3,2,1,0:T(8,128)S(1)}, f32[1,24,36,128]{3,2,1,0:T(8,128)S(1)}, u32[]{:S(2)}, u32[]{:S(2)}) collective-permute-start(f32[1,24,36,128]{3,2,1,0:T(8,128)S(1)} %get-tuple-element.36), channel_id=1, source_target_pairs={{0,1},{1,2},{2,3},{3,4},{4,5},{5,6},{6,7},{7,8},{8,9},{9,10},{10,1... | collective-permute-start | bytes 1327112 | tf_op jit(solution)/shard_map/ppermute | solution.py:28
  129.4 2.9 %fusion.100 = (f32[4,24,36,127]{3,2,1,0:T(8,128)S(1)}, f32[4,24,36,127]{3,2,1,0:T(8,128)S(1)}) fusion(f32[4,24,36,128]{3,2,1,0:T(8,128)} %get-tuple-element.12), kind=kLoop, calls=%fused_computation.145 | loop fusion | bytes 7022592 | tf_op jit(solution)/shard_map/slice | solution.py:119
  138.2 3.6 %collective-permute-start.12 = (f32[1,24,36,128]{3,2,1,0:T(8,128)S(1)}, f32[1,24,36,128]{3,2,1,0:T(8,128)S(1)}, u32[]{:S(2)}, u32[]{:S(2)}) collective-permute-start(f32[1,24,36,128]{3,2,1,0:T(8,128)S(1)} %get-tuple-element.32), channel_id=1, source_target_pairs={{0,1},{1,2},{2,3},{3,4},{4,5},{5,6},{6,7},{7,8},{8,9},{9,10},{10,1... | collective-permute-start | bytes 1327112 | tf_op jit(solution)/shard_map/ppermute | solution.py:28
  143.2 4.0 %collective-permute-start.18 = (f32[4,4,36,128]{3,2,1,0:T(8,128)S(1)}, f32[4,4,36,128]{3,2,1,0:T(8,128)S(1)}, u32[]{:S(2)}, u32[]{:S(2)}) collective-permute-start(f32[4,4,36,128]{3,2,1,0:T(8,128)S(1)} %get-tuple-element.24), channel_id=1, source_target_pairs={{0,16},{1,17},{2,18},{3,19},{4,20},{5,21},{6,22},{7,23},{8,24},{9,... | collective-permute-start | bytes 884744 | tf_op jit(solution)/shard_map/ppermute | solution.py:28
  147.8 4.0 %collective-permute-done.13 = f32[1,24,36,128]{3,2,1,0:T(8,128)S(1)} collective-permute-done((f32[1,24,36,128]{3,2,1,0:T(8,128)S(1)}, f32[1,24,36,128]{3,2,1,0:T(8,128)S(1)}, u32[]{:S(2)}, u32[]{:S(2)}) %collective-permute-start.13) | collective-permute-done | bytes 442400 | tf_op jit(solution)/shard_map/ppermute | solution.py:31
  155.8 3.6 %collective-permute-start.14 = (f32[1,24,36,128]{3,2,1,0:T(8,128)S(1)}, f32[1,24,36,128]{3,2,1,0:T(8,128)S(1)}, u32[]{:S(2)}, u32[]{:S(2)}) collective-permute-start(f32[1,24,36,128]{3,2,1,0:T(8,128)S(1)} %get-tuple-element.28), channel_id=1, source_target_pairs={{0,1},{1,2},{2,3},{3,4},{4,5},{5,6},{6,7},{7,8},{8,9},{9,10},{10,1... | collective-permute-start | bytes 1327112 | tf_op jit(solution)/shard_map/ppermute | solution.py:28
  160.6 7.3 %collective-permute-done.15 = f32[1,24,36,128]{3,2,1,0:T(8,128)S(1)} collective-permute-done((f32[1,24,36,128]{3,2,1,0:T(8,128)S(1)}, f32[1,24,36,128]{3,2,1,0:T(8,128)S(1)}, u32[]{:S(2)}, u32[]{:S(2)}) %collective-permute-start.15) | collective-permute-done | bytes 442400 | tf_op jit(solution)/shard_map/ppermute | solution.py:31
  167.9 4.9 %fusion.8 = f32[4,24,36,128]{3,2,1,0:T(8,128)S(1)} fusion(f32[4,24,36,128]{3,2,1,0:T(8,128)S(1)} %get-tuple-element.7, f32[4,24,36,128]{3,2,1,0:T(8,128)S(1)} %multiply_multiply_fusion, f32[1,24,36,128]{3,2,1,0:T(8,128)S(1)} %collective-permute-done.15, f32[1,24,36,128]{3,2,1,0:T(8,128)S(1)} %collective-permute-done.14, ...), kind=kLoop, calls=%fused_computation.27 | loop fusion | flops 15040512 | bytes 20375288 | tf_op jit(solution)/shard_map/mul | solution.py:158
  (101 shorter events, 50.3 us)
Async XLA Ops:
  1.3 8.7 %copy-start.12 = (s32[4]{0:T(128)S(1)}, s32[4]{0:T(128)}, u32[]{:S(2)}) copy-start(s32[4]{0:T(128)} %param.12) | copy-start | bytes 52
  1.3 12.6 %copy-start = (f32[4,24,36,128]{3,1,2,0:T(8,128)S(1)}, f32[4,24,36,128]{3,1,2,0:T(8,128)}, u32[]{:S(2)}) copy-start(f32[4,24,36,128]{3,1,2,0:T(8,128)} %param.7) | copy-start | bytes 5308420
  4.5 9.5 %copy-start.15 = (f32[2]{0:T(128)S(1)}, f32[2]{0:T(128)}, u32[]{:S(2)}) copy-start(f32[2]{0:T(128)} %param.13) | copy-start | bytes 28
  4.5 12.8 %copy-start.16 = (f32[4,128]{1,0:T(4,128)S(1)}, f32[4,128]{1,0:T(4,128)}, u32[]{:S(2)}) copy-start(f32[4,128]{1,0:T(4,128)} %param.8) | copy-start | bytes 6148
  4.6 13.0 %collective-permute-start.17 = (f32[4,4,36,128]{3,2,1,0:T(8,128)S(1)}, f32[4,4,36,128]{3,2,1,0:T(8,128)S(1)}, u32[]{:S(2)}, u32[]{:S(2)}) collective-permute-start(f32[4,4,36,128]{3,2,1,0:T(8,128)S(1)} %get-tuple-element.27), channel_id=1, source_target_pairs={{16,0},{17,1},{18,2},{19,3},{20,4},{21,5},{22,6},{23,7},{24,8},{25... | collective-permute-start | bytes 884744 | tf_op jit(solution)/shard_map/ppermute | solution.py:31
  5.9 11.7 %collective-permute-start.16 = (f32[4,4,36,128]{3,2,1,0:T(8,128)S(1)}, f32[4,4,36,128]{3,2,1,0:T(8,128)S(1)}, u32[]{:S(2)}, u32[]{:S(2)}) collective-permute-start(f32[4,4,36,128]{3,2,1,0:T(8,128)S(1)} %get-tuple-element.26), channel_id=1, source_target_pairs={{0,16},{1,17},{2,18},{3,19},{4,20},{5,21},{6,22},{7,23},{8,24},{9,... | collective-permute-start | bytes 884744 | tf_op jit(solution)/shard_map/ppermute | solution.py:28
  25.7 16.0 %collective-permute-start.1 = (f32[1,24,36,128]{3,2,1,0:T(8,128)S(1)}, f32[1,24,36,128]{3,2,1,0:T(8,128)S(1)}, u32[]{:S(2)}, u32[]{:S(2)}) collective-permute-start(f32[1,24,36,128]{3,2,1,0:T(8,128)S(1)} %get-tuple-element.57), channel_id=1, source_target_pairs={{1,0},{2,1},{3,2},{4,3},{5,4},{6,5},{7,6},{8,7},{9,8},{10,9},{11,1... | collective-permute-start | bytes 1327112 | tf_op jit(solution)/shard_map/ppermute | solution.py:31
  28.8 12.9 %collective-permute-start = (f32[1,24,36,128]{3,2,1,0:T(8,128)S(1)}, f32[1,24,36,128]{3,2,1,0:T(8,128)S(1)}, u32[]{:S(2)}, u32[]{:S(2)}) collective-permute-start(f32[1,24,36,128]{3,2,1,0:T(8,128)S(1)} %get-tuple-element.56), channel_id=1, source_target_pairs={{0,1},{1,2},{2,3},{3,4},{4,5},{5,6},{6,7},{7,8},{8,9},{9,10},{10,1... | collective-permute-start | bytes 1327112 | tf_op jit(solution)/shard_map/ppermute | solution.py:28
  44.0 15.8 %collective-permute-start.3 = (f32[1,24,36,128]{3,2,1,0:T(8,128)S(1)}, f32[1,24,36,128]{3,2,1,0:T(8,128)S(1)}, u32[]{:S(2)}, u32[]{:S(2)}) collective-permute-start(f32[1,24,36,128]{3,2,1,0:T(8,128)S(1)} %get-tuple-element.53), channel_id=1, source_target_pairs={{1,0},{2,1},{3,2},{4,3},{5,4},{6,5},{7,6},{8,7},{9,8},{10,9},{11,1... | collective-permute-start | bytes 1327112 | tf_op jit(solution)/shard_map/ppermute | solution.py:31
  45.9 13.8 %collective-permute-start.2 = (f32[1,24,36,128]{3,2,1,0:T(8,128)S(1)}, f32[1,24,36,128]{3,2,1,0:T(8,128)S(1)}, u32[]{:S(2)}, u32[]{:S(2)}) collective-permute-start(f32[1,24,36,128]{3,2,1,0:T(8,128)S(1)} %get-tuple-element.52), channel_id=1, source_target_pairs={{0,1},{1,2},{2,3},{3,4},{4,5},{5,6},{6,7},{7,8},{8,9},{9,10},{10,1... | collective-permute-start | bytes 1327112 | tf_op jit(solution)/shard_map/ppermute | solution.py:28
  61.7 15.1 %collective-permute-start.5 = (f32[1,24,36,128]{3,2,1,0:T(8,128)S(1)}, f32[1,24,36,128]{3,2,1,0:T(8,128)S(1)}, u32[]{:S(2)}, u32[]{:S(2)}) collective-permute-start(f32[1,24,36,128]{3,2,1,0:T(8,128)S(1)} %get-tuple-element.49), channel_id=1, source_target_pairs={{1,0},{2,1},{3,2},{4,3},{5,4},{6,5},{7,6},{8,7},{9,8},{10,9},{11,1... | collective-permute-start | bytes 1327112 | tf_op jit(solution)/shard_map/ppermute | solution.py:31
  63.6 13.2 %collective-permute-start.4 = (f32[1,24,36,128]{3,2,1,0:T(8,128)S(1)}, f32[1,24,36,128]{3,2,1,0:T(8,128)S(1)}, u32[]{:S(2)}, u32[]{:S(2)}) collective-permute-start(f32[1,24,36,128]{3,2,1,0:T(8,128)S(1)} %get-tuple-element.48), channel_id=1, source_target_pairs={{0,1},{1,2},{2,3},{3,4},{4,5},{5,6},{6,7},{7,8},{8,9},{9,10},{10,1... | collective-permute-start | bytes 1327112 | tf_op jit(solution)/shard_map/ppermute | solution.py:28
  78.7 14.7 %collective-permute-start.7 = (f32[1,24,36,128]{3,2,1,0:T(8,128)S(1)}, f32[1,24,36,128]{3,2,1,0:T(8,128)S(1)}, u32[]{:S(2)}, u32[]{:S(2)}) collective-permute-start(f32[1,24,36,128]{3,2,1,0:T(8,128)S(1)} %get-tuple-element.45), channel_id=1, source_target_pairs={{1,0},{2,1},{3,2},{4,3},{5,4},{6,5},{7,6},{8,7},{9,8},{10,9},{11,1... | collective-permute-start | bytes 1327112 | tf_op jit(solution)/shard_map/ppermute | solution.py:31
  80.6 12.8 %collective-permute-start.6 = (f32[1,24,36,128]{3,2,1,0:T(8,128)S(1)}, f32[1,24,36,128]{3,2,1,0:T(8,128)S(1)}, u32[]{:S(2)}, u32[]{:S(2)}) collective-permute-start(f32[1,24,36,128]{3,2,1,0:T(8,128)S(1)} %get-tuple-element.44), channel_id=1, source_target_pairs={{0,1},{1,2},{2,3},{3,4},{4,5},{5,6},{6,7},{7,8},{8,9},{9,10},{10,1... | collective-permute-start | bytes 1327112 | tf_op jit(solution)/shard_map/ppermute | solution.py:28
  98.7 14.4 %collective-permute-start.9 = (f32[1,24,36,128]{3,2,1,0:T(8,128)}, f32[1,24,36,128]{3,2,1,0:T(8,128)S(1)}, u32[]{:S(2)}, u32[]{:S(2)}) collective-permute-start(f32[1,24,36,128]{3,2,1,0:T(8,128)} %get-tuple-element.41), channel_id=1, source_target_pairs={{1,0},{2,1},{3,2},{4,3},{5,4},{6,5},{7,6},{8,7},{9,8},{10,9},{11,1... | collective-permute-start | bytes 1327112 | tf_op jit(solution)/shard_map/ppermute | solution.py:31
  100.7 12.4 %collective-permute-start.8 = (f32[1,24,36,128]{3,2,1,0:T(8,128)S(1)}, f32[1,24,36,128]{3,2,1,0:T(8,128)S(1)}, u32[]{:S(2)}, u32[]{:S(2)}) collective-permute-start(f32[1,24,36,128]{3,2,1,0:T(8,128)S(1)} %get-tuple-element.40), channel_id=1, source_target_pairs={{0,1},{1,2},{2,3},{3,4},{4,5},{5,6},{6,7},{7,8},{8,9},{9,10},{10,1... | collective-permute-start | bytes 1327112 | tf_op jit(solution)/shard_map/ppermute | solution.py:28
  118.5 15.6 %collective-permute-start.11 = (f32[1,24,36,128]{3,2,1,0:T(8,128)}, f32[1,24,36,128]{3,2,1,0:T(8,128)S(1)}, u32[]{:S(2)}, u32[]{:S(2)}) collective-permute-start(f32[1,24,36,128]{3,2,1,0:T(8,128)} %get-tuple-element.37), channel_id=1, source_target_pairs={{1,0},{2,1},{3,2},{4,3},{5,4},{6,5},{7,6},{8,7},{9,8},{10,9},{11,1... | collective-permute-start | bytes 1327112 | tf_op jit(solution)/shard_map/ppermute | solution.py:31
  120.4 13.7 %collective-permute-start.10 = (f32[1,24,36,128]{3,2,1,0:T(8,128)S(1)}, f32[1,24,36,128]{3,2,1,0:T(8,128)S(1)}, u32[]{:S(2)}, u32[]{:S(2)}) collective-permute-start(f32[1,24,36,128]{3,2,1,0:T(8,128)S(1)} %get-tuple-element.36), channel_id=1, source_target_pairs={{0,1},{1,2},{2,3},{3,4},{4,5},{5,6},{6,7},{7,8},{8,9},{9,10},{10,1... | collective-permute-start | bytes 1327112 | tf_op jit(solution)/shard_map/ppermute | solution.py:28
  136.1 15.8 %collective-permute-start.13 = (f32[1,24,36,128]{3,2,1,0:T(8,128)S(1)}, f32[1,24,36,128]{3,2,1,0:T(8,128)S(1)}, u32[]{:S(2)}, u32[]{:S(2)}) collective-permute-start(f32[1,24,36,128]{3,2,1,0:T(8,128)S(1)} %get-tuple-element.33), channel_id=1, source_target_pairs={{1,0},{2,1},{3,2},{4,3},{5,4},{6,5},{7,6},{8,7},{9,8},{10,9},{11,1... | collective-permute-start | bytes 1327112 | tf_op jit(solution)/shard_map/ppermute | solution.py:31
  138.2 13.7 %collective-permute-start.12 = (f32[1,24,36,128]{3,2,1,0:T(8,128)S(1)}, f32[1,24,36,128]{3,2,1,0:T(8,128)S(1)}, u32[]{:S(2)}, u32[]{:S(2)}) collective-permute-start(f32[1,24,36,128]{3,2,1,0:T(8,128)S(1)} %get-tuple-element.32), channel_id=1, source_target_pairs={{0,1},{1,2},{2,3},{3,4},{4,5},{5,6},{6,7},{7,8},{8,9},{9,10},{10,1... | collective-permute-start | bytes 1327112 | tf_op jit(solution)/shard_map/ppermute | solution.py:28
  141.9 17.5 %collective-permute-start.19 = (f32[4,4,36,128]{3,2,1,0:T(8,128)S(1)}, f32[4,4,36,128]{3,2,1,0:T(8,128)S(1)}, u32[]{:S(2)}, u32[]{:S(2)}) collective-permute-start(f32[4,4,36,128]{3,2,1,0:T(8,128)S(1)} %get-tuple-element.25), channel_id=1, source_target_pairs={{16,0},{17,1},{18,2},{19,3},{20,4},{21,5},{22,6},{23,7},{24,8},{25... | collective-permute-start | bytes 884744 | tf_op jit(solution)/shard_map/ppermute | solution.py:31
  143.2 16.2 %collective-permute-start.18 = (f32[4,4,36,128]{3,2,1,0:T(8,128)S(1)}, f32[4,4,36,128]{3,2,1,0:T(8,128)S(1)}, u32[]{:S(2)}, u32[]{:S(2)}) collective-permute-start(f32[4,4,36,128]{3,2,1,0:T(8,128)S(1)} %get-tuple-element.24), channel_id=1, source_target_pairs={{0,16},{1,17},{2,18},{3,19},{4,20},{5,21},{6,22},{7,23},{8,24},{9,... | collective-permute-start | bytes 884744 | tf_op jit(solution)/shard_map/ppermute | solution.py:28
  153.8 14.1 %collective-permute-start.15 = (f32[1,24,36,128]{3,2,1,0:T(8,128)S(1)}, f32[1,24,36,128]{3,2,1,0:T(8,128)S(1)}, u32[]{:S(2)}, u32[]{:S(2)}) collective-permute-start(f32[1,24,36,128]{3,2,1,0:T(8,128)S(1)} %get-tuple-element.29), channel_id=1, source_target_pairs={{1,0},{2,1},{3,2},{4,3},{5,4},{6,5},{7,6},{8,7},{9,8},{10,9},{11,1... | collective-permute-start | bytes 1327112 | tf_op jit(solution)/shard_map/ppermute | solution.py:31
  155.8 12.1 %collective-permute-start.14 = (f32[1,24,36,128]{3,2,1,0:T(8,128)S(1)}, f32[1,24,36,128]{3,2,1,0:T(8,128)S(1)}, u32[]{:S(2)}, u32[]{:S(2)}) collective-permute-start(f32[1,24,36,128]{3,2,1,0:T(8,128)S(1)} %get-tuple-element.28), channel_id=1, source_target_pairs={{0,1},{1,2},{2,3},{3,4},{4,5},{5,6},{6,7},{7,8},{8,9},{9,10},{10,1... | collective-permute-start | bytes 1327112 | tf_op jit(solution)/shard_map/ppermute | solution.py:28
  (13 other events, 54.0 us)
where the time goes:
time: 176 us; the launch traced here: 174 us
  starting transfers between devices  56.2 us (32%)
  waiting for transfers between devices  50.8 us (29%)
  other arithmetic  32.2 us (18%)
  local copies, waits for them, and re-layouts  19.4 us (11%)
  between operations  11.7 us (7%)
  blocking collectives  3.97 us (2%)
    ppermute x10, waiting for transfers between devices, padded(): lax.ppermute(lax.slice_in_dim(block, 0, width, axis=dim), axis, backward)  50.8 us
    ppermute x10, starting transfers between devices, padded(): lax.ppermute(lax.slice_in_dim(block, block.shape[dim] - width, None, axis...  36.9 us
    ppermute x10, starting transfers between devices, padded(): lax.ppermute(lax.slice_in_dim(block, 0, width, axis=dim), axis, backward)  19.3 us
    mul x7, other arithmetic, body(): east_flux = east_speed * spectrum  13.2 us
    slice x8, local copies, waits for them, and re-layouts, east_west(): behind = jnp.concatenate([zeros, east_flux[..., :-1]], axis=-1)  9.6 us
    unnamed x35, local copies, waits for them, and re-layouts  6.24 us
    mul x1, other arithmetic, interaction(): coupling * (masked * masked * (coef_plus * upper + coef_minus * lower) -...  5.35 us
    mul x1, other arithmetic, body(): return (wet_four * (spectrum + increment), orbital)  4.89 us
  transfers between devices with their start and end apart: 20, of which 8 were waited for; matrix products, arithmetic and copies ran while one was open for 8% of the time, Pallas kernels for 0%

commit v1 on v0

--- a/solution.py
+++ b/solution.py
@@ -1,8 +1,12 @@
+import functools
 import math
 
 import jax
 import jax.numpy as jnp
+import numpy as np
 from jax import lax
+from jax.experimental import pallas as pl
+from jax.experimental.pallas import tpu as pltpu
 from jax.sharding import PartitionSpec as P
 
 FH = 4
@@ -122,7 +126,7 @@
     return east_going * (east_flux - behind) + (1.0 - east_going) * (ahead - east_flux)
 
 
-def body(energy, water_depth, wet_mask, vegetation, canopy, quad_offsets, quad_weights):
+def plain_body(energy, water_depth, wet_mask, vegetation, canopy, quad_offsets, quad_weights):
     tile_rows, freq_count, dir_count, tile_cols = energy.shape
     wet_field = wet_mask.astype(jnp.float32)
     veg_field = vegetation.astype(jnp.float32)
@@ -158,6 +162,395 @@
     return (wet_four * (spectrum + increment), orbital)
 
 
+MESH = pl.DeviceIdType.MESH
+ROWS = 4
+REACH = 8
+PART = 3
+
+
+def sinh_of(x):
+    square = x * x
+    series = 1.0 + square / 210.0
+    for term in (156.0, 110.0, 72.0, 42.0, 20.0, 6.0):
+        series = 1.0 + square / term * series
+    wide = jnp.exp(x)
+    return jnp.where(x < 1.7, x * series, 0.5 * (wide - 1.0 / wide))
+
+
+def tanh_of(x):
+    low = sinh_of(jnp.minimum(x, 1.0))
+    fall = jnp.exp(-2.0 * x)
+    return jnp.where(x < 1.0, low / jnp.sqrt(1.0 + low * low), (1.0 - fall) / (1.0 + fall))
+
+
+def kernel(
+    groups,
+    tiles,
+    dirs,
+    quad_offsets,
+    quad_weights,
+    coefs,
+    energy,
+    radian,
+    depth,
+    wet_mask,
+    vegetation,
+    canopy,
+    out,
+    orbital,
+    ext,
+    quads,
+    spec,
+    incr,
+    inbox,
+    outbox,
+    fringe,
+    speed,
+    wet,
+    drag,
+    part_mine,
+    part_theirs,
+    send_sem,
+    recv_sem,
+    fringe_sems,
+    part_sems,
+):
+    bins = energy.shape[2]
+    quarter = dirs // 4
+    parts = quarter // PART
+    mine = lax.axis_index("freq")
+    tile = lax.axis_index("geo")
+    has_below = tile > 0
+    has_above = tile < tiles - 1
+    below_id = jnp.maximum(tile - 1, 0)
+    above_id = jnp.minimum(tile + 1, tiles - 1)
+
+    barrier = pltpu.get_barrier_semaphore()
+    pl.semaphore_signal(barrier, inc=1, device_id=(1 - mine, tile), device_id_type=MESH)
+
+    @pl.when(has_below)
+    def _():
+        pl.semaphore_signal(barrier, inc=1, device_id=(mine, below_id), device_id_type=MESH)
+
+    @pl.when(has_above)
+    def _():
+        pl.semaphore_signal(barrier, inc=1, device_id=(mine, above_id), device_id_type=MESH)
+
+    first = pl.multiple_of(mine * bins, 8)
+    freq = radian[pl.ds(first, bins), :]
+    square = freq * freq
+    for row in range(ROWS):
+        column = jnp.broadcast_to(depth[row : row + 1, :], (bins, 128))
+        ratio = square * column / gravity
+        wave = ratio / jnp.sqrt(tanh_of(ratio))
+        speed[row] = (sub_step / cell_size) * (
+            freq * column / wave * (0.5 + wave / sinh_of(2.0 * wave))
+        )
+        wet[row] = jnp.broadcast_to(wet_mask[row : row + 1, :].astype(jnp.float32), (bins, 128))
+
+    def edge(step, q, k):
+        first_dir = q * quarter + k * PART
+        north = q < 2
+        return pltpu.make_async_remote_copy(
+            src_ref=outbox.at[step, pl.ds(first_dir, PART)],
+            dst_ref=inbox.at[step, pl.ds(first_dir, PART)],
+            send_sem=send_sem.at[step, q, k],
+            recv_sem=recv_sem.at[step, q, k],
+            device_id=(mine, above_id if north else below_id),
+            device_id_type=MESH,
+        )
+
+    def sends(q):
+        return has_above if q < 2 else has_below
+
+    def receives(q):
+        return has_below if q < 2 else has_above
+
+    waits = 1 + has_below.astype(jnp.int32) + has_above.astype(jnp.int32)
+    pl.semaphore_wait(barrier, waits)
+
+    def first_edges(k, carry):
+        for q in (0, 2, 1, 3):
+            row = ROWS - 1 if q < 2 else 0
+            for d in range(PART):
+                j = q * quarter + k * PART + d
+                outbox[0, j] = speed[row] * (wet[row] * energy[j, row])
+
+            @pl.when(sends(q))
+            def _():
+                edge(0, q, k).start()
+
+        return carry
+
+    lax.fori_loop(0, parts, first_edges, 0)
+
+    fringe_copy = pltpu.make_async_remote_copy(
+        src_ref=energy.at[:, :, pl.ds(pl.multiple_of((1 - mine) * (bins - REACH), 8), REACH), :],
+        dst_ref=fringe,
+        send_sem=fringe_sems.at[0],
+        recv_sem=fringe_sems.at[1],
+        device_id=(1 - mine, tile),
+        device_id_type=MESH,
+    )
+    fringe_copy.start()
+
+    @pl.when(jnp.logical_not(has_below))
+    def _():
+        def clear(step, carry):
+            inbox[step, pl.ds(0, 2 * quarter)] = jnp.zeros((2 * quarter, bins, 128), jnp.float32)
+            return carry
+
+        lax.fori_loop(0, SUBSTEPS, clear, 0)
+
+    @pl.when(jnp.logical_not(has_above))
+    def _():
+        def clear(step, carry):
+            inbox[step, pl.ds(2 * quarter, 2 * quarter)] = jnp.zeros(
+                (2 * quarter, bins, 128), jnp.float32
+            )
+            return carry
+
+        lax.fori_loop(0, SUBSTEPS, clear, 0)
+
+    empty = pl.multiple_of(mine * (REACH + bins), 8)
+    taken = pl.multiple_of((1 - mine) * (REACH + bins), 8)
+
+    def fill(j, totals):
+        sums = []
+        for row in range(ROWS):
+            raw = energy[j, row]
+            wetted = wet[row] * raw
+            spec[j, row] = wetted
+            ext[j, row, REACH : REACH + bins, :] = wetted
+            ext[j, row, pl.ds(empty, REACH), :] = jnp.zeros((REACH, 128), jnp.float32)
+            sums.append(totals[row] + raw)
+        return tuple(sums)
+
+    totals = lax.fori_loop(
+        0, dirs, fill, tuple(jnp.zeros((bins, 128), jnp.float32) for _ in range(ROWS))
+    )
+    for row in range(ROWS):
+        column = jnp.broadcast_to(depth[row : row + 1, :], (bins, 128))
+        ratio = square * column / gravity
+        wave = ratio / jnp.sqrt(tanh_of(ratio))
+        steep = sinh_of(wave)
+        weight = (
+            square / (steep * steep) * (freq * (freq_ratio - 1.0)) * (2.0 * math.pi / dirs)
+        )
+        part_mine[row] = jnp.broadcast_to(
+            jnp.sum(weight * totals[row], axis=0, keepdims=True), (8, 128)
+        )
+    part_copy = pltpu.make_async_remote_copy(
+        src_ref=part_mine,
+        dst_ref=part_theirs,
+        send_sem=part_sems.at[0],
+        recv_sem=part_sems.at[1],
+        device_id=(1 - mine, tile),
+        device_id_type=MESH,
+    )
+    part_copy.start()
+
+    lane = lax.broadcasted_iota(jnp.int32, (bins, 128), 1)
+
+    def move(step, q, k, last):
+        east = q in (0, 3)
+        north = q < 2
+        inside = (lane != (0 if east else 127)).astype(jnp.float32)
+        order = range(ROWS) if north else range(ROWS - 1, -1, -1)
+        for d in range(PART):
+            j = q * quarter + k * PART + d
+            across, along = coefs[0, j], coefs[1, j]
+            both = across + along
+            sideways = across * inside
+            before = inbox[step, j]
+            for row in order:
+                held = spec[j, row]
+                flux = speed[row] * held
+                beside = pltpu.roll(flux, 1 if east else 127, 1)
+                fresh = wet[row] * (held - both * flux + sideways * beside + along * before)
+                before = flux
+                if last:
+                    out[j, row] = fresh + wet[row] * incr[j, row]
+                else:
+                    spec[j, row] = fresh
+            if not last:
+                outbox[step + 1, j] = speed[row] * fresh
+
+    def substep(step, last=False):
+        def piece(k, carry):
+            for q in (0, 2, 1, 3):
+
+                @pl.when(receives(q))
+                def _():
+                    edge(step, q, k).wait_recv()
+
+                move(step, q, k, last)
+                if not last:
+
+                    @pl.when(sends(q))
+                    def _():
+                        edge(step + 1, q, k).start()
+
+            return carry
+
+        lax.fori_loop(0, parts, piece, 0)
+
+    def plain_step(step, carry):
+        substep(step)
+        return carry
+
+    lax.fori_loop(0, 3, plain_step, 0)
+
+    part_copy.wait()
+    fringe_copy.wait()
+
+    for row in range(ROWS):
+        total = jnp.sqrt(part_mine[row] + part_theirs[row])
+        orbital[row : row + 1, :] = total[0:1, :]
+        leaves = vegetation[row : row + 1, :].astype(jnp.float32) * canopy[row : row + 1, :]
+        damping = 1.0 + (SUBSTEPS * sub_step) * leaves * total[0:1, :]
+        drag[row] = jnp.broadcast_to(1.0 / damping, (bins, 128))
+
+    def take(j, carry):
+        for row in range(ROWS):
+            ext[j, row, pl.ds(taken, REACH), :] = wet[row, 0:REACH, :] * fringe[j, row]
+        return carry
+
+    lax.fori_loop(0, dirs, take, 0)
+
+    up_bins, up_turn, down_turn = quad_offsets[0], quad_offsets[2], quad_offsets[3]
+    weight_up, weight_down = quad_weights[0], quad_weights[1]
+    rest_up, rest_down = 1.0 - weight_up, 1.0 - weight_down
+    half = REACH // 2
+    span = bins + REACH
+
+    def turned(j, turn):
+        j = j + turn
+        j = jnp.where(j >= dirs, j - dirs, j)
+        return jnp.where(j < 0, j + dirs, j)
+
+    def couple(j, carry):
+        high, low = turned(j, up_turn), turned(j, -down_turn)
+        for row in range(ROWS):
+            here = ext[j, row, half : half + span, :]
+            upper = (
+                weight_up * ext[high, row, pl.ds(half + up_bins, span), :]
+                + rest_up * ext[high, row, pl.ds(half + up_bins + 1, span), :]
+            )
+            lower = (
+                weight_down * ext[low, row, half - 3 : half - 3 + span, :]
+                + rest_down * ext[low, row, half - 4 : half - 4 + span, :]
+            )
+            quads[j, row] = (coupling * here) * (
+                here * (coef_plus * upper + coef_minus * lower) - coef_both * (upper * lower)
+            )
+        return carry
+
+    def spread(j, carry):
+        back, ahead = turned(j, -up_turn), turned(j, down_turn)
+        for row in range(ROWS):
+            change = (
+                weight_up * quads[back, row, pl.ds(half - up_bins, bins), :]
+                + rest_up * quads[back, row, pl.ds(half - up_bins - 1, bins), :]
+                + weight_down * quads[ahead, row, half + 3 : half + 3 + bins, :]
+                + rest_down * quads[ahead, row, half + 4 : half + 4 + bins, :]
+                - 2.0 * quads[j, row, half : half + bins, :]
+            )
+            wetted = ext[j, row, REACH : REACH + bins, :]
+            incr[j, row] = (wetted + (SUBSTEPS * sub_step) * change) * drag[row] - wetted
+        return carry
+
+    def couple_step(step, carry):
+        substep(step)
+        lax.fori_loop((step - 3) * (dirs // 2), (step - 2) * (dirs // 2), couple, 0)
+        return carry
+
+    def spread_step(step, carry):
+        substep(step)
+        lax.fori_loop((step - 5) * (dirs // 2), (step - 4) * (dirs // 2), spread, 0)
+        return carry
+
+    lax.fori_loop(3, 5, couple_step, 0)
+    lax.fori_loop(5, 7, spread_step, 0)
+    substep(SUBSTEPS - 1, last=True)
+
+    def drain(step, carry):
+        def piece(k, inner):
+            for q in range(4):
+
+                @pl.when(sends(q))
+                def _():
+                    edge(step, q, k).wait_send()
+
+            return inner
+
+        return lax.fori_loop(0, parts, piece, carry)
+
+    lax.fori_loop(0, SUBSTEPS, drain, 0)
+
+
+def kernel_body(groups, tiles, energy, water_depth, wet_mask, vegetation, canopy, offsets, weights):
+    rows, bins, dirs, cols = energy.shape
+    angles = (np.arange(dirs, dtype=np.float32) + np.float32(0.5)) * np.float32(
+        2.0 * math.pi / dirs
+    )
+    coefs = np.abs(np.stack([np.cos(angles), np.sin(angles)])).astype(np.float32)
+    radian = 2.0 * math.pi * base_freq * freq_ratio ** np.arange(groups * bins)
+    radian = np.broadcast_to(radian.astype(np.float32)[:, None], (groups * bins, cols))
+    vmem = pl.BlockSpec(memory_space=pltpu.VMEM)
+    smem = pl.BlockSpec(memory_space=pltpu.SMEM)
+    f32 = jnp.float32
+    parts = dirs // 4 // PART
+    moved, orbital = pl.pallas_call(
+        functools.partial(kernel, groups, tiles, dirs),
+        out_shape=(
+            jax.ShapeDtypeStruct((dirs, rows, bins, cols), f32),
+            jax.ShapeDtypeStruct((rows, cols), f32),
+        ),
+        in_specs=[smem] * 3 + [vmem] * 6,
+        out_specs=(vmem, vmem),
+        scratch_shapes=[
+            pltpu.VMEM((dirs, rows, bins + 2 * REACH, cols), f32),
+            pltpu.VMEM((dirs, rows, bins + REACH, cols), f32),
+            pltpu.VMEM((dirs, rows, bins, cols), f32),
+            pltpu.VMEM((dirs, rows, bins, cols), f32),
+            pltpu.VMEM((SUBSTEPS, dirs, bins, cols), f32),
+            pltpu.VMEM((SUBSTEPS, dirs, bins, cols), f32),
+            pltpu.VMEM((dirs, rows, REACH, cols), f32),
+            pltpu.VMEM((rows, bins, cols), f32),
+            pltpu.VMEM((rows, bins, cols), f32),
+            pltpu.VMEM((rows, bins, cols), f32),
+            pltpu.VMEM((rows, 8, cols), f32),
+            pltpu.VMEM((rows, 8, cols), f32),
+            pltpu.SemaphoreType.DMA((SUBSTEPS, 4, parts)),
+            pltpu.SemaphoreType.DMA((SUBSTEPS, 4, parts)),
+            pltpu.SemaphoreType.DMA((2,)),
+            pltpu.SemaphoreType.DMA((2,)),
+        ],
+        compiler_params=pltpu.CompilerParams(
+            collective_id=0, has_side_effects=True, vmem_limit_bytes=48 * 1024 * 1024
+        ),
+    )(
+        offsets,
+        weights,
+        jnp.asarray(coefs),
+        jnp.transpose(energy, (2, 0, 1, 3)),
+        jnp.asarray(radian),
+        water_depth,
+        wet_mask,
+        vegetation,
+        canopy,
+    )
+    return jnp.transpose(moved, (1, 2, 0, 3)), orbital
+
+
+def body(groups, tiles, energy, *rest):
+    rows, bins, dirs, cols = energy.shape
+    if groups == 2 and rows == ROWS and bins % 8 == 0 and dirs % (4 * PART) == 0 and cols == 128:
+        return kernel_body(groups, tiles, energy, *rest)
+    return plain_body(energy, *rest)
+
+
 def solution(mesh):
     placed = (
         P("geo", "freq", None, None),
@@ -169,7 +562,7 @@
         P(),
     )
     return jax.shard_map(
-        body,
+        functools.partial(body, mesh.shape["freq"], mesh.shape["geo"]),
         mesh=mesh,
         in_specs=placed,
         out_specs=(P("geo", "freq", None, None), P("geo", None)),

time: 176 us -> 51.1 us (0.29)
  starting transfers between devices: 56.2 us -> 0 us
  waiting for transfers between devices: 50.8 us -> 0 us
  Pallas kernels: 0 us -> 46.4 us
  other arithmetic: 32.2 us -> 0 us
  local copies, waits for them, and re-layouts: 19.4 us -> 3.75 us
  between operations: 11.7 us -> 0.76 us
  blocking collectives: 3.97 us -> 0 us
    ppermute x20 -> x0, starting transfers between devices: 56.2 us -> none  [the longest x10 36.9 us: padded(): lax.ppermute(lax.slice_in_dim(block, block.shape[dim] - width, None, axis...]
    ppermute x20 -> x0, waiting for transfers between devices: 50.8 us -> none  [the longest x10 50.8 us: padded(): lax.ppermute(lax.slice_in_dim(block, 0, width, axis=dim), axis, backward)]
    pallas_call x0 -> x1, Pallas kernels: none -> 46.4 us  [kernel_body(): pl.pallas_call(functools.partial(kernel, groups, tiles, dirs), out_shape=...]
    mul x19 -> x0, other arithmetic: 27.3 us -> none  [the longest x7 13.2 us: body(): east_flux = east_speed * spectrum]
    slice x20 -> x0, local copies, waits for them, and re-layouts: 13.2 us -> none  [the longest x8 9.6 us: east_west(): behind = jnp.concatenate([zeros, east_flux[..., :-1]], axis=-1)]
    psum x1 -> x0, blocking collectives: 3.97 us -> none  [body(): orbital = jnp.sqrt(lax.psum(partial_value, 'freq'))]
    concatenate x2 -> x0, other arithmetic: 3.18 us -> none  [the longest x1 2.62 us: interaction(): doubled = jnp.concatenate([extended, extended], axis=2)]
    unnamed x35 -> x19, local copies, waits for them, and re-layouts: 6.24 us -> 3.68 us
  transfers between devices with their start and end apart: 20 -> 0, of which waited for: 8 -> 0; matrix products, arithmetic and copies ran while one was open for 8% -> 0% of each run, Pallas kernels for 0% -> 0%
where the time goes in v1:
time: 51.1 us; the launch traced here: 50.9 us
  Pallas kernels  46.4 us (91%)
  local copies, waits for them, and re-layouts  3.75 us (7%)
  between operations  0.76 us (1%)
    pallas_call x1, Pallas kernels, kernel_body(): pl.pallas_call(functools.partial(kernel, groups, tiles, dirs), out_shape=...  46.4 us
    unnamed x19, local copies, waits for them, and re-layouts  3.68 us

profile of v1, /device:TPU:17, one launch (start us, length us, event | category | flops | bytes accessed | tf_op | source)
XLA Modules:
  0.0 50.9 jit_solution(6352262488859727180)
XLA Ops:
  0.6 0.0 copy-start.7
  0.6 0.0 copy-start.4
  0.7 0.0 copy-start.6
  0.7 0.0 copy-start.5
  0.7 0.0 copy-start.3
  0.7 0.0 copy-start.2
  0.7 0.0 copy-start.1
  0.7 0.0 copy-start
  0.7 1.7 %copy.14 = f32[4,24,36,128]{3,1,0,2:T(8,128)S(1)} copy(f32[4,24,36,128]{3,1,2,0:T(8,128)} %param.9) | data formatting | bytes 3538944 | tf_op args[0]
  2.5 0.0 copy-done.7
  2.5 0.1 jit_solution_.3.radian
  2.5 0.0 copy-done.4
  2.5 0.0 copy-done.6
  2.5 0.0 copy-done.5
  2.6 0.0 copy-done.3
  2.6 0.0 copy-done.2
  2.6 0.0 copy-done.1
  2.6 0.0 copy-done
  2.6 46.4 %shard_map.104 = (f32[36,4,24,128]{3,2,1,0:T(8,128)S(1)}, f32[4,128]{1,0:T(4,128)S(1)}) custom-call(s32[4]{0:T(128)S(1)} %copy-done.5, f32[2]{0:T(128)S(1)} %copy-done.6, f32[2,36]{1,0:T(2,128)S(1)} %copy-done.4, f32[36,4,24,128]{3,2,1,0:T(8,128)S(1)} %bitcast.4, f32[48,128]{1,0:T(8,128)S(1)} %jit_solution_.3.radian, f32[4,128]{1,0:T(4,128)S(1)} %copy-done, ...), custom_call_target="tpu_custom_call" | custom-call | tf_op jit(solution)/shard_map/pallas_call | solution.py:504
  49.0 1.3 %copy.12 = f32[4,24,36,128]{3,1,2,0:T(8,128)} copy(f32[4,24,36,128]{3,1,0,2:T(8,128)S(1)} %bitcast.5) | data formatting | bytes 3538944
  50.3 0.6 %copy.16 = f32[4,128]{1,0:T(4,128)} copy(f32[4,128]{1,0:T(4,128)S(1)} %get-tuple-element.11) | data formatting | bytes 4096
Async XLA Ops:
  0.6 1.8 %copy-start.7 = (f32[48]{0:T(128)S(1)}, f32[48]{0:T(128)}, u32[]{:S(2)}) copy-start(f32[48]{0:T(128)} %constant.5.clone) | copy-start | bytes 580
  0.6 1.9 %copy-start.4 = (f32[2,36]{1,0:T(2,128)S(1)}, f32[2,36]{1,0:T(2,128)}, u32[]{:S(2)}) copy-start(f32[2,36]{1,0:T(2,128)} %constant.4.clone.coefs) | copy-start | bytes 868
  0.7 1.9 %copy-start.6 = (f32[2]{0:T(128)S(1)}, f32[2]{0:T(128)}, u32[]{:S(2)}) copy-start(f32[2]{0:T(128)} %quad_weights.1) | copy-start | bytes 28
  0.7 1.9 %copy-start.5 = (s32[4]{0:T(128)S(1)}, s32[4]{0:T(128)}, u32[]{:S(2)}) copy-start(s32[4]{0:T(128)} %quad_offsets.1) | copy-start | bytes 52
  0.7 1.9 %copy-start.3 = (f32[4,128]{1,0:T(4,128)S(1)}, f32[4,128]{1,0:T(4,128)}, u32[]{:S(2)}) copy-start(f32[4,128]{1,0:T(4,128)} %canopy.1) | copy-start | bytes 6148
  0.7 1.9 %copy-start.2 = (s32[4,128]{1,0:T(4,128)S(1)}, s32[4,128]{1,0:T(4,128)}, u32[]{:S(2)}) copy-start(s32[4,128]{1,0:T(4,128)} %vegetation.1) | copy-start | bytes 6148
  0.7 1.9 %copy-start.1 = (s32[4,128]{1,0:T(4,128)S(1)}, s32[4,128]{1,0:T(4,128)}, u32[]{:S(2)}) copy-start(s32[4,128]{1,0:T(4,128)} %wet_mask.1) | copy-start | bytes 6148
  0.7 1.9 %copy-start = (f32[4,128]{1,0:T(4,128)S(1)}, f32[4,128]{1,0:T(4,128)}, u32[]{:S(2)}) copy-start(f32[4,128]{1,0:T(4,128)} %depth.1) | copy-start | bytes 6148

commit v2 on v1

--- a/solution.py
+++ b/solution.py
@@ -198,13 +198,14 @@
     canopy,
     out,
     orbital,
+    loaded,
+    stored,
     ext,
     quads,
     spec,
     incr,
     inbox,
     outbox,
-    fringe,
     speed,
     wet,
     drag,
@@ -214,8 +215,10 @@
     recv_sem,
     fringe_sems,
     part_sems,
+    load_sem,
+    store_sem,
 ):
-    bins = energy.shape[2]
+    bins = energy.shape[1]
     quarter = dirs // 4
     parts = quarter // PART
     mine = lax.axis_index("freq")
@@ -224,6 +227,12 @@
     has_above = tile < tiles - 1
     below_id = jnp.maximum(tile - 1, 0)
     above_id = jnp.minimum(tile + 1, tiles - 1)
+
+    def load(row):
+        return pltpu.make_async_copy(energy.at[row], loaded.at[row], load_sem.at[row])
+
+    for row in (ROWS - 1, 0, *range(1, ROWS - 1)):
+        load(row).start()
 
     barrier = pltpu.get_barrier_semaphore()
     pl.semaphore_signal(barrier, inc=1, device_id=(1 - mine, tile), device_id_type=MESH)
@@ -266,15 +275,31 @@
     def receives(q):
         return has_below if q < 2 else has_above
 
-    waits = 1 + has_below.astype(jnp.int32) + has_above.astype(jnp.int32)
-    pl.semaphore_wait(barrier, waits)
+
+    empty = pl.multiple_of(mine * (REACH + bins), 8)
+    leaving = pl.multiple_of(REACH + (1 - mine) * (bins - REACH), 8)
+
+    def fill(row):
+        load(row).wait()
+        total = jnp.zeros((bins, 128), jnp.float32)
+        for base in range(0, dirs, 8):
+            count = min(8, dirs - base)
+            raw = jnp.swapaxes(loaded[row, :, base : base + count, :], 0, 1)
+            total = total + jnp.sum(raw, axis=0)
+            wetted = wet[row][None] * raw
+            spec[base : base + count, row] = wetted
+            ext[base : base + count, row, REACH : REACH + bins, :] = wetted
+            ext[base : base + count, row, pl.ds(empty, REACH), :] = jnp.zeros(
+                (count, REACH, 128), jnp.float32
+            )
+        return total
 
     def first_edges(k, carry):
         for q in (0, 2, 1, 3):
             row = ROWS - 1 if q < 2 else 0
             for d in range(PART):
                 j = q * quarter + k * PART + d
-                outbox[0, j] = speed[row] * (wet[row] * energy[j, row])
+                outbox[0, j] = speed[row] * spec[j, row]
 
             @pl.when(sends(q))
             def _():
@@ -282,17 +307,26 @@
 
         return carry
 
+    totals = {row: fill(row) for row in (ROWS - 1, 0)}
+    waits = 1 + has_below.astype(jnp.int32) + has_above.astype(jnp.int32)
+    pl.semaphore_wait(barrier, waits)
     lax.fori_loop(0, parts, first_edges, 0)
-
-    fringe_copy = pltpu.make_async_remote_copy(
-        src_ref=energy.at[:, :, pl.ds(pl.multiple_of((1 - mine) * (bins - REACH), 8), REACH), :],
-        dst_ref=fringe,
-        send_sem=fringe_sems.at[0],
-        recv_sem=fringe_sems.at[1],
-        device_id=(1 - mine, tile),
-        device_id_type=MESH,
-    )
-    fringe_copy.start()
+    for row in range(1, ROWS - 1):
+        totals[row] = fill(row)
+
+    pieces = 3 * parts
+    width = dirs // pieces
+
+    def fringe_copy(piece):
+        some = pl.ds(piece * width, width)
+        return pltpu.make_async_remote_copy(
+            src_ref=ext.at[some, :, pl.ds(leaving, REACH), :],
+            dst_ref=ext.at[some, :, pl.ds(empty, REACH), :],
+            send_sem=fringe_sems.at[0, piece],
+            recv_sem=fringe_sems.at[1, piece],
+            device_id=(1 - mine, tile),
+            device_id_type=MESH,
+        )
 
     @pl.when(jnp.logical_not(has_below))
     def _():
@@ -312,23 +346,6 @@
 
         lax.fori_loop(0, SUBSTEPS, clear, 0)
 
-    empty = pl.multiple_of(mine * (REACH + bins), 8)
-    taken = pl.multiple_of((1 - mine) * (REACH + bins), 8)
-
-    def fill(j, totals):
-        sums = []
-        for row in range(ROWS):
-            raw = energy[j, row]
-            wetted = wet[row] * raw
-            spec[j, row] = wetted
-            ext[j, row, REACH : REACH + bins, :] = wetted
-            ext[j, row, pl.ds(empty, REACH), :] = jnp.zeros((REACH, 128), jnp.float32)
-            sums.append(totals[row] + raw)
-        return tuple(sums)
-
-    totals = lax.fori_loop(
-        0, dirs, fill, tuple(jnp.zeros((bins, 128), jnp.float32) for _ in range(ROWS))
-    )
     for row in range(ROWS):
         column = jnp.broadcast_to(depth[row : row + 1, :], (bins, 128))
         ratio = square * column / gravity
@@ -370,39 +387,54 @@
                 fresh = wet[row] * (held - both * flux + sideways * beside + along * before)
                 before = flux
                 if last:
-                    out[j, row] = fresh + wet[row] * incr[j, row]
+                    spec[j, row] = fresh + wet[row] * incr[j, row]
                 else:
                     spec[j, row] = fresh
             if not last:
                 outbox[step + 1, j] = speed[row] * fresh
 
-    def substep(step, last=False):
-        def piece(k, carry):
-            for q in (0, 2, 1, 3):
-
-                @pl.when(receives(q))
-                def _():
-                    edge(step, q, k).wait_recv()
-
-                move(step, q, k, last)
-                if not last:
-
-                    @pl.when(sends(q))
+    def substep(step, extra=None, last=False):
+        for near, far in ((0, 2), (1, 3)):
+
+            def piece(k, carry, near=near, far=far):
+                for q in (near, far):
+
+                    @pl.when(receives(q))
                     def _():
-                        edge(step + 1, q, k).start()
-
-            return carry
-
-        lax.fori_loop(0, parts, piece, 0)
-
-    def plain_step(step, carry):
-        substep(step)
+                        edge(step, q, k).wait_recv()
+
+                    move(step, q, k, last)
+                    if not last:
+
+                        @pl.when(sends(q))
+                        def _():
+                            edge(step + 1, q, k).start()
+
+                if extra is not None:
+                    extra((near % 2) * parts + k)
+                return carry
+
+            lax.fori_loop(0, parts, piece, 0)
+
+    def early_step(step, carry):
+        def extra(n):
+            @pl.when(n < parts)
+            def _():
+                fringe_copy(step * parts + n).start()
+
+        substep(step, extra)
         return carry
 
-    lax.fori_loop(0, 3, plain_step, 0)
+    lax.fori_loop(0, 3, early_step, 0)
+    substep(3)
 
     part_copy.wait()
-    fringe_copy.wait()
+
+    def fringe_wait(piece, carry):
+        fringe_copy(piece).wait()
+        return carry
+
+    lax.fori_loop(0, pieces, fringe_wait, 0)
 
     for row in range(ROWS):
         total = jnp.sqrt(part_mine[row] + part_theirs[row])
@@ -410,13 +442,6 @@
         leaves = vegetation[row : row + 1, :].astype(jnp.float32) * canopy[row : row + 1, :]
         damping = 1.0 + (SUBSTEPS * sub_step) * leaves * total[0:1, :]
         drag[row] = jnp.broadcast_to(1.0 / damping, (bins, 128))
-
-    def take(j, carry):
-        for row in range(ROWS):
-            ext[j, row, pl.ds(taken, REACH), :] = wet[row, 0:REACH, :] * fringe[j, row]
-        return carry
-
-    lax.fori_loop(0, dirs, take, 0)
 
     up_bins, up_turn, down_turn = quad_offsets[0], quad_offsets[2], quad_offsets[3]
     weight_up, weight_down = quad_weights[0], quad_weights[1]
@@ -461,18 +486,33 @@
         return carry
 
     def couple_step(step, carry):
-        substep(step)
-        lax.fori_loop((step - 3) * (dirs // 2), (step - 2) * (dirs // 2), couple, 0)
+        share = dirs // (4 * parts)
+
+        def extra(n):
+            first_dir = ((step - 4) * 2 * parts + n) * share
+            lax.fori_loop(first_dir, first_dir + share, couple, 0)
+
+        substep(step, extra)
         return carry
 
-    def spread_step(step, carry):
-        substep(step)
-        lax.fori_loop((step - 5) * (dirs // 2), (step - 4) * (dirs // 2), spread, 0)
-        return carry
-
-    lax.fori_loop(3, 5, couple_step, 0)
-    lax.fori_loop(5, 7, spread_step, 0)
+    def spread_some(n):
+        share = dirs // (2 * parts)
+        lax.fori_loop(n * share, (n + 1) * share, spread, 0)
+
+    lax.fori_loop(4, 6, couple_step, 0)
+    substep(SUBSTEPS - 2, spread_some)
     substep(SUBSTEPS - 1, last=True)
+
+    def store(row):
+        return pltpu.make_async_copy(stored.at[row], out.at[row], store_sem.at[row])
+
+    for row in range(ROWS):
+        for base in range(0, dirs, 8):
+            count = min(8, dirs - base)
+            stored[row, :, base : base + count, :] = jnp.swapaxes(
+                spec[base : base + count, row], 0, 1
+            )
+        store(row).start()
 
     def drain(step, carry):
         def piece(k, inner):
@@ -487,6 +527,8 @@
         return lax.fori_loop(0, parts, piece, carry)
 
     lax.fori_loop(0, SUBSTEPS, drain, 0)
+    for row in range(ROWS):
+        store(row).wait()
 
 
 def kernel_body(groups, tiles, energy, water_depth, wet_mask, vegetation, canopy, offsets, weights):
@@ -504,19 +546,20 @@
     moved, orbital = pl.pallas_call(
         functools.partial(kernel, groups, tiles, dirs),
         out_shape=(
-            jax.ShapeDtypeStruct((dirs, rows, bins, cols), f32),
+            jax.ShapeDtypeStruct((rows, bins, dirs, cols), f32),
             jax.ShapeDtypeStruct((rows, cols), f32),
         ),
-        in_specs=[smem] * 3 + [vmem] * 6,
-        out_specs=(vmem, vmem),
+        in_specs=[smem] * 3 + [pl.BlockSpec(memory_space=pl.ANY)] + [vmem] * 5,
+        out_specs=(pl.BlockSpec(memory_space=pl.ANY), vmem),
         scratch_shapes=[
+            pltpu.VMEM((rows, bins, dirs, cols), f32),
+            pltpu.VMEM((rows, bins, dirs, cols), f32),
             pltpu.VMEM((dirs, rows, bins + 2 * REACH, cols), f32),
             pltpu.VMEM((dirs, rows, bins + REACH, cols), f32),
             pltpu.VMEM((dirs, rows, bins, cols), f32),
             pltpu.VMEM((dirs, rows, bins, cols), f32),
             pltpu.VMEM((SUBSTEPS, dirs, bins, cols), f32),
             pltpu.VMEM((SUBSTEPS, dirs, bins, cols), f32),
-            pltpu.VMEM((dirs, rows, REACH, cols), f32),
             pltpu.VMEM((rows, bins, cols), f32),
             pltpu.VMEM((rows, bins, cols), f32),
             pltpu.VMEM((rows, bins, cols), f32),
@@ -524,8 +567,10 @@
             pltpu.VMEM((rows, 8, cols), f32),
             pltpu.SemaphoreType.DMA((SUBSTEPS, 4, parts)),
             pltpu.SemaphoreType.DMA((SUBSTEPS, 4, parts)),
+            pltpu.SemaphoreType.DMA((2, 3 * parts)),
             pltpu.SemaphoreType.DMA((2,)),
-            pltpu.SemaphoreType.DMA((2,)),
+            pltpu.SemaphoreType.DMA((rows,)),
+            pltpu.SemaphoreType.DMA((rows,)),
         ],
         compiler_params=pltpu.CompilerParams(
             collective_id=0, has_side_effects=True, vmem_limit_bytes=48 * 1024 * 1024
@@ -534,14 +579,14 @@
         offsets,
         weights,
         jnp.asarray(coefs),
-        jnp.transpose(energy, (2, 0, 1, 3)),
+        energy,
         jnp.asarray(radian),
         water_depth,
         wet_mask,
         vegetation,
         canopy,
     )
-    return jnp.transpose(moved, (1, 2, 0, 3)), orbital
+    return moved, orbital
 
 
 def body(groups, tiles, energy, *rest):

time: 51.1 us -> 53.1 us (1.039)
  Pallas kernels: 46.4 us -> 48.1 us
    pallas_call x1, Pallas kernels: 46.4 us -> 48.1 us  [kernel_body(): pl.pallas_call(functools.partial(kernel, groups, tiles, dirs), out_shape=...]
    pallas_call x0 -> x1, local copies, waits for them, and re-layouts: none -> 1.52 us  [kernel_body(): pl.pallas_call(functools.partial(kernel, groups, tiles, dirs), out_shape=...]
    unnamed x19 -> x18, local copies, waits for them, and re-layouts: 3.68 us -> 2.46 us
where the time goes in v2:
time: 53.1 us; the launch traced here: 52.9 us
  Pallas kernels  48.1 us (91%)
  local copies, waits for them, and re-layouts  4.06 us (8%)
  between operations  0.75 us (1%)
    pallas_call x1, Pallas kernels, kernel_body(): pl.pallas_call(functools.partial(kernel, groups, tiles, dirs), out_shape=...  48.1 us
    unnamed x18, local copies, waits for them, and re-layouts  2.46 us
    pallas_call x1, local copies, waits for them, and re-layouts, kernel_body(): pl.pallas_call(functools.partial(kernel, groups, tiles, dirs), out_shape=...  1.52 us

profile of v2, /device:TPU:17, one launch (start us, length us, event | category | flops | bytes accessed | tf_op | source)
XLA Modules:
  0.0 52.9 jit_solution(4886974664964340094)
XLA Ops:
  0.6 0.0 copy-start.4
  0.6 0.0 copy-start.7
  0.7 0.0 copy-start.6
  0.7 0.0 copy-start.5
  0.7 0.0 copy-start.3
  0.7 0.0 copy-start.2
  0.7 0.0 copy-start.1
  0.7 0.0 copy-start
  0.7 1.8 %copy.11.energy = f32[4,24,36,128]{3,2,1,0:T(8,128)S(1)} copy(f32[4,24,36,128]{3,1,2,0:T(8,128)} %param.9) | data formatting | bytes 3538944 | tf_op args[0]
  2.6 0.0 copy-done.7
  2.6 0.1 jit_solution_.3.radian
  2.6 0.0 copy-done.4
  2.7 0.0 copy-done.6
  2.7 0.0 copy-done.5
  2.7 0.0 copy-done.3
  2.7 0.0 copy-done.2
  2.7 0.0 copy-done.1
  2.7 0.0 copy-done
  2.7 48.1 %shard_map.104 = (f32[4,24,36,128]{3,2,1,0:T(8,128)S(1)}, f32[4,128]{1,0:T(4,128)S(1)}) custom-call(s32[4]{0:T(128)S(1)} %copy-done.5, f32[2]{0:T(128)S(1)} %copy-done.6, f32[2,36]{1,0:T(2,128)S(1)} %copy-done.4, f32[4,24,36,128]{3,2,1,0:T(8,128)S(1)} %copy.11.energy, f32[48,128]{1,0:T(8,128)S(1)} %jit_solution_.3.radian, f32[4,128]{1,0:T(4,128)S(1)} %copy-done, ...), custom_call_target="tpu_custom_call" | custom-call | tf_op jit(solution)/shard_map/pallas_call | solution.py:546
  50.8 1.5 %copy.12 = f32[4,24,36,128]{3,1,2,0:T(8,128)} copy(f32[4,24,36,128]{3,2,1,0:T(8,128)S(1)} %get-tuple-element.2) | data formatting | bytes 3538944 | tf_op jit(solution)/shard_map/pallas_call | solution.py:546
  52.3 0.6 %copy.14 = f32[4,128]{1,0:T(4,128)} copy(f32[4,128]{1,0:T(4,128)S(1)} %get-tuple-element.7) | data formatting | bytes 4096
Async XLA Ops:
  0.6 2.0 %copy-start.4 = (f32[2,36]{1,0:T(2,128)S(1)}, f32[2,36]{1,0:T(2,128)}, u32[]{:S(2)}) copy-start(f32[2,36]{1,0:T(2,128)} %constant.4.clone.coefs) | copy-start | bytes 868
  0.6 1.9 %copy-start.7 = (f32[48]{0:T(128)S(1)}, f32[48]{0:T(128)}, u32[]{:S(2)}) copy-start(f32[48]{0:T(128)} %constant.5.clone) | copy-start | bytes 580
  0.7 2.0 %copy-start.6 = (f32[2]{0:T(128)S(1)}, f32[2]{0:T(128)}, u32[]{:S(2)}) copy-start(f32[2]{0:T(128)} %quad_weights.1) | copy-start | bytes 28
  0.7 2.0 %copy-start.5 = (s32[4]{0:T(128)S(1)}, s32[4]{0:T(128)}, u32[]{:S(2)}) copy-start(s32[4]{0:T(128)} %quad_offsets.1) | copy-start | bytes 52
  0.7 2.0 %copy-start.3 = (f32[4,128]{1,0:T(4,128)S(1)}, f32[4,128]{1,0:T(4,128)}, u32[]{:S(2)}) copy-start(f32[4,128]{1,0:T(4,128)} %canopy.1) | copy-start | bytes 6148
  0.7 2.0 %copy-start.2 = (s32[4,128]{1,0:T(4,128)S(1)}, s32[4,128]{1,0:T(4,128)}, u32[]{:S(2)}) copy-start(s32[4,128]{1,0:T(4,128)} %vegetation.1) | copy-start | bytes 6148
  0.7 2.0 %copy-start.1 = (s32[4,128]{1,0:T(4,128)S(1)}, s32[4,128]{1,0:T(4,128)}, u32[]{:S(2)}) copy-start(s32[4,128]{1,0:T(4,128)} %wet_mask.1) | copy-start | bytes 6148
  0.7 2.0 %copy-start = (f32[4,128]{1,0:T(4,128)S(1)}, f32[4,128]{1,0:T(4,128)}, u32[]{:S(2)}) copy-start(f32[4,128]{1,0:T(4,128)} %depth.1) | copy-start | bytes 6148

commit v3 on v2

--- a/solution.py
+++ b/solution.py
@@ -215,10 +215,12 @@
     recv_sem,
     fringe_sems,
     part_sems,
+    orbit_row,
     load_sem,
     store_sem,
+    orbit_sem,
 ):
-    bins = energy.shape[1]
+    bins = energy.shape[2]
     quarter = dirs // 4
     parts = quarter // PART
     mine = lax.axis_index("freq")
@@ -228,11 +230,16 @@
     below_id = jnp.maximum(tile - 1, 0)
     above_id = jnp.minimum(tile + 1, tiles - 1)
 
-    def load(row):
-        return pltpu.make_async_copy(energy.at[row], loaded.at[row], load_sem.at[row])
-
-    for row in (ROWS - 1, 0, *range(1, ROWS - 1)):
-        load(row).start()
+    def load(row, side):
+        some = pl.ds(side * 2 * quarter, 2 * quarter)
+        return pltpu.make_async_copy(
+            energy.at[row, some], loaded.at[row, some], load_sem.at[row, side]
+        )
+
+    urgent = ((ROWS - 1, 0), (0, 1))
+    later = [(row, side) for row in range(ROWS) for side in range(2) if (row, side) not in urgent]
+    for row, side in (*urgent, *later):
+        load(row, side).start()
 
     barrier = pltpu.get_barrier_semaphore()
     pl.semaphore_signal(barrier, inc=1, device_id=(1 - mine, tile), device_id_type=MESH)
@@ -279,27 +286,12 @@
     empty = pl.multiple_of(mine * (REACH + bins), 8)
     leaving = pl.multiple_of(REACH + (1 - mine) * (bins - REACH), 8)
 
-    def fill(row):
-        load(row).wait()
-        total = jnp.zeros((bins, 128), jnp.float32)
-        for base in range(0, dirs, 8):
-            count = min(8, dirs - base)
-            raw = jnp.swapaxes(loaded[row, :, base : base + count, :], 0, 1)
-            total = total + jnp.sum(raw, axis=0)
-            wetted = wet[row][None] * raw
-            spec[base : base + count, row] = wetted
-            ext[base : base + count, row, REACH : REACH + bins, :] = wetted
-            ext[base : base + count, row, pl.ds(empty, REACH), :] = jnp.zeros(
-                (count, REACH, 128), jnp.float32
-            )
-        return total
-
     def first_edges(k, carry):
         for q in (0, 2, 1, 3):
             row = ROWS - 1 if q < 2 else 0
             for d in range(PART):
                 j = q * quarter + k * PART + d
-                outbox[0, j] = speed[row] * spec[j, row]
+                outbox[0, j] = speed[row] * (wet[row] * loaded[row, j])
 
             @pl.when(sends(q))
             def _():
@@ -307,12 +299,28 @@
 
         return carry
 
-    totals = {row: fill(row) for row in (ROWS - 1, 0)}
+    for row, side in urgent:
+        load(row, side).wait()
     waits = 1 + has_below.astype(jnp.int32) + has_above.astype(jnp.int32)
     pl.semaphore_wait(barrier, waits)
     lax.fori_loop(0, parts, first_edges, 0)
-    for row in range(1, ROWS - 1):
-        totals[row] = fill(row)
+    for row, side in later:
+        load(row, side).wait()
+
+    def fill(j, totals):
+        sums = []
+        for row in range(ROWS):
+            raw = loaded[row, j]
+            wetted = wet[row] * raw
+            spec[j, row] = wetted
+            ext[j, row, REACH : REACH + bins, :] = wetted
+            ext[j, row, pl.ds(empty, REACH), :] = jnp.zeros((REACH, 128), jnp.float32)
+            sums.append(totals[row] + raw)
+        return tuple(sums)
+
+    totals = lax.fori_loop(
+        0, dirs, fill, tuple(jnp.zeros((bins, 128), jnp.float32) for _ in range(ROWS))
+    )
 
     pieces = 3 * parts
     width = dirs // pieces
@@ -387,12 +395,16 @@
                 fresh = wet[row] * (held - both * flux + sideways * beside + along * before)
                 before = flux
                 if last:
-                    spec[j, row] = fresh + wet[row] * incr[j, row]
+                    stored[row, j] = fresh + wet[row] * incr[j, row]
                 else:
                     spec[j, row] = fresh
             if not last:
                 outbox[step + 1, j] = speed[row] * fresh
 
+    def store(q, k):
+        some = pl.ds(q * quarter + k * PART, PART)
+        return pltpu.make_async_copy(stored.at[:, some], out.at[:, some], store_sem.at[q, k])
+
     def substep(step, extra=None, last=False):
         for near, far in ((0, 2), (1, 3)):
 
@@ -404,7 +416,9 @@
                         edge(step, q, k).wait_recv()
 
                     move(step, q, k, last)
-                    if not last:
+                    if last:
+                        store(q, k).start()
+                    else:
 
                         @pl.when(sends(q))
                         def _():
@@ -438,11 +452,13 @@
 
     for row in range(ROWS):
         total = jnp.sqrt(part_mine[row] + part_theirs[row])
-        orbital[row : row + 1, :] = total[0:1, :]
+        orbit_row[row : row + 1, :] = total[0:1, :]
         leaves = vegetation[row : row + 1, :].astype(jnp.float32) * canopy[row : row + 1, :]
         damping = 1.0 + (SUBSTEPS * sub_step) * leaves * total[0:1, :]
         drag[row] = jnp.broadcast_to(1.0 / damping, (bins, 128))
 
+    orbit_copy = pltpu.make_async_copy(orbit_row, orbital, orbit_sem)
+    orbit_copy.start()
     up_bins, up_turn, down_turn = quad_offsets[0], quad_offsets[2], quad_offsets[3]
     weight_up, weight_down = quad_weights[0], quad_weights[1]
     rest_up, rest_down = 1.0 - weight_up, 1.0 - weight_down
@@ -503,17 +519,6 @@
     substep(SUBSTEPS - 2, spread_some)
     substep(SUBSTEPS - 1, last=True)
 
-    def store(row):
-        return pltpu.make_async_copy(stored.at[row], out.at[row], store_sem.at[row])
-
-    for row in range(ROWS):
-        for base in range(0, dirs, 8):
-            count = min(8, dirs - base)
-            stored[row, :, base : base + count, :] = jnp.swapaxes(
-                spec[base : base + count, row], 0, 1
-            )
-        store(row).start()
-
     def drain(step, carry):
         def piece(k, inner):
             for q in range(4):
@@ -527,8 +532,14 @@
         return lax.fori_loop(0, parts, piece, carry)
 
     lax.fori_loop(0, SUBSTEPS, drain, 0)
-    for row in range(ROWS):
-        store(row).wait()
+    orbit_copy.wait()
+
+    def finish(k, carry):
+        for q in range(4):
+            store(q, k).wait()
+        return carry
+
+    lax.fori_loop(0, parts, finish, 0)
 
 
 def kernel_body(groups, tiles, energy, water_depth, wet_mask, vegetation, canopy, offsets, weights):
@@ -540,20 +551,21 @@
     radian = 2.0 * math.pi * base_freq * freq_ratio ** np.arange(groups * bins)
     radian = np.broadcast_to(radian.astype(np.float32)[:, None], (groups * bins, cols))
     vmem = pl.BlockSpec(memory_space=pltpu.VMEM)
+    hbm = pl.BlockSpec(memory_space=pltpu.HBM)
     smem = pl.BlockSpec(memory_space=pltpu.SMEM)
     f32 = jnp.float32
     parts = dirs // 4 // PART
     moved, orbital = pl.pallas_call(
         functools.partial(kernel, groups, tiles, dirs),
         out_shape=(
-            jax.ShapeDtypeStruct((rows, bins, dirs, cols), f32),
+            jax.ShapeDtypeStruct((rows, dirs, bins, cols), f32),
             jax.ShapeDtypeStruct((rows, cols), f32),
         ),
-        in_specs=[smem] * 3 + [pl.BlockSpec(memory_space=pl.ANY)] + [vmem] * 5,
-        out_specs=(pl.BlockSpec(memory_space=pl.ANY), vmem),
+        in_specs=[smem] * 3 + [hbm] + [vmem] * 5,
+        out_specs=(hbm, hbm),
         scratch_shapes=[
-            pltpu.VMEM((rows, bins, dirs, cols), f32),
-            pltpu.VMEM((rows, bins, dirs, cols), f32),
+            pltpu.VMEM((rows, dirs, bins, cols), f32),
+            pltpu.VMEM((rows, dirs, bins, cols), f32),
             pltpu.VMEM((dirs, rows, bins + 2 * REACH, cols), f32),
             pltpu.VMEM((dirs, rows, bins + REACH, cols), f32),
             pltpu.VMEM((dirs, rows, bins, cols), f32),
@@ -569,8 +581,10 @@
             pltpu.SemaphoreType.DMA((SUBSTEPS, 4, parts)),
             pltpu.SemaphoreType.DMA((2, 3 * parts)),
             pltpu.SemaphoreType.DMA((2,)),
-            pltpu.SemaphoreType.DMA((rows,)),
-            pltpu.SemaphoreType.DMA((rows,)),
+            pltpu.VMEM((rows, cols), f32),
+            pltpu.SemaphoreType.DMA((rows, 2)),
+            pltpu.SemaphoreType.DMA((4, parts)),
+            pltpu.SemaphoreType.DMA(()),
         ],
         compiler_params=pltpu.CompilerParams(
             collective_id=0, has_side_effects=True, vmem_limit_bytes=48 * 1024 * 1024
@@ -579,14 +593,14 @@
         offsets,
         weights,
         jnp.asarray(coefs),
-        energy,
+        jnp.swapaxes(energy, 1, 2),
         jnp.asarray(radian),
         water_depth,
         wet_mask,
         vegetation,
         canopy,
     )
-    return moved, orbital
+    return jnp.swapaxes(moved, 1, 2), orbital
 
 
 def body(groups, tiles, energy, *rest):

time: 53.1 us -> 59.6 us (1.12)
  local copies, waits for them, and re-layouts: 4.06 us -> 8.71 us
  Pallas kernels: 48.1 us -> 49.9 us
    unnamed x18, local copies, waits for them, and re-layouts: 2.46 us -> 7.98 us
    pallas_call x1, Pallas kernels: 48.1 us -> 49.9 us  [kernel_body(): pl.pallas_call(functools.partial(kernel, groups, tiles, dirs), out_shape=...]
    pallas_call x1 -> x0, local copies, waits for them, and re-layouts: 1.52 us -> none  [kernel_body(): pl.pallas_call(functools.partial(kernel, groups, tiles, dirs), out_shape=...]
    another operation x1, local copies, waits for them, and re-layouts: 0.07 us -> 0.73 us
where the time goes in v3:
time: 59.6 us; the launch traced here: 59.3 us
  Pallas kernels  49.9 us (84%)
  local copies, waits for them, and re-layouts  8.71 us (15%)
  between operations  0.65 us (1%)
    pallas_call x1, Pallas kernels, kernel_body(): pl.pallas_call(functools.partial(kernel, groups, tiles, dirs), out_shape=...  49.9 us
    unnamed x18, local copies, waits for them, and re-layouts  7.98 us

profile of v3, /device:TPU:17, one launch (start us, length us, event | category | flops | bytes accessed | tf_op | source)
XLA Modules:
  0.0 59.3 jit_solution(6989662364089632264)
XLA Ops:
  0.6 0.7 %jit_solution_.3.radian = f32[48,128]{1,0:T(8,128)S(1)} broadcast(f32[48]{0:T(128)} %constant.5.clone), dimensions={0} | broadcast | bytes 24768 | tf_op jit(solution)
  1.4 0.0 copy-start
  1.4 1.5 %copy-done = f32[4,24,36,128]{3,1,2,0:T(8,128)S(1)} copy-done((f32[4,24,36,128]{3,1,2,0:T(8,128)S(1)}, f32[4,24,36,128]{3,1,2,0:T(8,128)}, u32[]{:S(2)}) %copy-start) | copy-done | bytes 1769496
  2.8 0.0 copy-start.1
  2.8 0.7 %copy-done.1 = f32[4,128]{1,0:T(4,128)S(1)} copy-done((f32[4,128]{1,0:T(4,128)S(1)}, f32[4,128]{1,0:T(4,128)}, u32[]{:S(2)}) %copy-start.1) | copy-done | bytes 2072
  3.5 0.0 copy-start.2
  3.5 0.7 %copy-done.2 = s32[4,128]{1,0:T(4,128)S(1)} copy-done((s32[4,128]{1,0:T(4,128)S(1)}, s32[4,128]{1,0:T(4,128)}, u32[]{:S(2)}) %copy-start.2) | copy-done | bytes 2072
  4.2 0.0 copy-start.3
  4.2 0.7 %copy-done.3 = s32[4,128]{1,0:T(4,128)S(1)} copy-done((s32[4,128]{1,0:T(4,128)S(1)}, s32[4,128]{1,0:T(4,128)}, u32[]{:S(2)}) %copy-start.3) | copy-done | bytes 2072
  4.9 0.0 copy-start.4
  4.9 0.7 %copy-done.4 = f32[4,128]{1,0:T(4,128)S(1)} copy-done((f32[4,128]{1,0:T(4,128)S(1)}, f32[4,128]{1,0:T(4,128)}, u32[]{:S(2)}) %copy-start.4) | copy-done | bytes 2072
  5.6 0.0 copy-start.5
  5.6 0.7 %copy-done.5 = f32[2,36]{1,0:T(2,128)S(1)} copy-done((f32[2,36]{1,0:T(2,128)S(1)}, f32[2,36]{1,0:T(2,128)}, u32[]{:S(2)}) %copy-start.5) | copy-done | bytes 312
  6.2 0.0 copy-start.6
  6.2 0.7 %copy-done.6 = s32[4]{0:T(128)S(1)} copy-done((s32[4]{0:T(128)S(1)}, s32[4]{0:T(128)}, u32[]{:S(2)}) %copy-start.6) | copy-done | bytes 40
  6.9 0.0 copy-start.7
  6.9 0.7 %copy-done.7 = f32[2]{0:T(128)S(1)} copy-done((f32[2]{0:T(128)S(1)}, f32[2]{0:T(128)}, u32[]{:S(2)}) %copy-start.7) | copy-done | bytes 32
  7.6 49.9 %shard_map.104 = (f32[4,36,24,128]{3,2,1,0:T(8,128)S(1)}, f32[4,128]{1,0:T(4,128)S(1)}) custom-call(s32[4]{0:T(128)S(1)} %copy-done.6, f32[2]{0:T(128)S(1)} %copy-done.7, f32[2,36]{1,0:T(2,128)S(1)} %copy-done.5, f32[4,36,24,128]{3,2,1,0:T(8,128)S(1)} %bitcast.3, f32[48,128]{1,0:T(8,128)S(1)} %jit_solution_.3.radian, f32[4,128]{1,0:T(4,128)S(1)} %copy-done.1, ...), custom_call_target="tpu_custom_call" | custom-call | tf_op jit(solution)/shard_map/pallas_call | solution.py:558
  57.5 1.2 %copy.13 = f32[4,24,36,128]{3,1,2,0:T(8,128)} copy(f32[4,24,36,128]{3,1,2,0:T(8,128)S(1)} %bitcast.2) | data formatting | bytes 3538944
  58.7 0.6 copy.14
Async XLA Ops:
  1.4 1.5 %copy-start = (f32[4,24,36,128]{3,1,2,0:T(8,128)S(1)}, f32[4,24,36,128]{3,1,2,0:T(8,128)}, u32[]{:S(2)}) copy-start(f32[4,24,36,128]{3,1,2,0:T(8,128)} %param.9) | copy-start | bytes 5308420
  2.8 0.7 %copy-start.1 = (f32[4,128]{1,0:T(4,128)S(1)}, f32[4,128]{1,0:T(4,128)}, u32[]{:S(2)}) copy-start(f32[4,128]{1,0:T(4,128)} %depth.1) | copy-start | bytes 6148
  3.5 0.7 %copy-start.2 = (s32[4,128]{1,0:T(4,128)S(1)}, s32[4,128]{1,0:T(4,128)}, u32[]{:S(2)}) copy-start(s32[4,128]{1,0:T(4,128)} %wet_mask.1) | copy-start | bytes 6148
  4.2 0.7 %copy-start.3 = (s32[4,128]{1,0:T(4,128)S(1)}, s32[4,128]{1,0:T(4,128)}, u32[]{:S(2)}) copy-start(s32[4,128]{1,0:T(4,128)} %vegetation.1) | copy-start | bytes 6148
  4.9 0.7 %copy-start.4 = (f32[4,128]{1,0:T(4,128)S(1)}, f32[4,128]{1,0:T(4,128)}, u32[]{:S(2)}) copy-start(f32[4,128]{1,0:T(4,128)} %canopy.1) | copy-start | bytes 6148
  5.6 0.7 %copy-start.5 = (f32[2,36]{1,0:T(2,128)S(1)}, f32[2,36]{1,0:T(2,128)}, u32[]{:S(2)}) copy-start(f32[2,36]{1,0:T(2,128)} %constant.4.clone.coefs) | copy-start | bytes 868
  6.2 0.7 %copy-start.6 = (s32[4]{0:T(128)S(1)}, s32[4]{0:T(128)}, u32[]{:S(2)}) copy-start(s32[4]{0:T(128)} %quad_offsets.1) | copy-start | bytes 52
  6.9 0.7 %copy-start.7 = (f32[2]{0:T(128)S(1)}, f32[2]{0:T(128)}, u32[]{:S(2)}) copy-start(f32[2]{0:T(128)} %quad_weights.1) | copy-start | bytes 28

commit v4 on v3

--- a/solution.py
+++ b/solution.py
@@ -3,7 +3,6 @@
 
 import jax
 import jax.numpy as jnp
-import numpy as np
 from jax import lax
 from jax.experimental import pallas as pl
 from jax.experimental.pallas import tpu as pltpu
@@ -189,13 +188,11 @@
     dirs,
     quad_offsets,
     quad_weights,
-    coefs,
     energy,
-    radian,
-    depth,
-    wet_mask,
-    vegetation,
-    canopy,
+    depth_in,
+    wet_in,
+    vegetation_in,
+    canopy_in,
     out,
     orbital,
     loaded,
@@ -216,6 +213,12 @@
     fringe_sems,
     part_sems,
     orbit_row,
+    coefs,
+    depth,
+    wet_mask,
+    vegetation,
+    canopy,
+    field_sem,
     load_sem,
     store_sem,
     orbit_sem,
@@ -238,6 +241,14 @@
 
     urgent = ((ROWS - 1, 0), (0, 1))
     later = [(row, side) for row in range(ROWS) for side in range(2) if (row, side) not in urgent]
+    fields = [
+        pltpu.make_async_copy(source, target, field_sem.at[at])
+        for at, (source, target) in enumerate(
+            ((depth_in, depth), (wet_in, wet_mask), (vegetation_in, vegetation), (canopy_in, canopy))
+        )
+    ]
+    for field in fields:
+        field.start()
     for row, side in (*urgent, *later):
         load(row, side).start()
 
@@ -252,9 +263,18 @@
     def _():
         pl.semaphore_signal(barrier, inc=1, device_id=(mine, above_id), device_id_type=MESH)
 
-    first = pl.multiple_of(mine * bins, 8)
-    freq = radian[pl.ds(first, bins), :]
+    for j in range(dirs):
+        angle = (j + 0.5) * 2.0 * math.pi / dirs
+        coefs[0, j] = jnp.float32(abs(math.cos(angle)))
+        coefs[1, j] = jnp.float32(abs(math.sin(angle)))
+    bin_index = lax.broadcasted_iota(jnp.int32, (bins, 128), 0) + mine * bins
+    freq = jnp.full((bins, 128), 2.0 * math.pi * base_freq, jnp.float32)
+    for bit in range((groups * bins - 1).bit_length()):
+        chosen = jnp.bitwise_and(bin_index, 1 << bit) > 0
+        freq = jnp.where(chosen, freq * (freq_ratio ** (1 << bit)), freq)
     square = freq * freq
+    for field in fields:
+        field.wait()
     for row in range(ROWS):
         column = jnp.broadcast_to(depth[row : row + 1, :], (bins, 128))
         ratio = square * column / gravity
@@ -544,13 +564,6 @@
 
 def kernel_body(groups, tiles, energy, water_depth, wet_mask, vegetation, canopy, offsets, weights):
     rows, bins, dirs, cols = energy.shape
-    angles = (np.arange(dirs, dtype=np.float32) + np.float32(0.5)) * np.float32(
-        2.0 * math.pi / dirs
-    )
-    coefs = np.abs(np.stack([np.cos(angles), np.sin(angles)])).astype(np.float32)
-    radian = 2.0 * math.pi * base_freq * freq_ratio ** np.arange(groups * bins)
-    radian = np.broadcast_to(radian.astype(np.float32)[:, None], (groups * bins, cols))
-    vmem = pl.BlockSpec(memory_space=pltpu.VMEM)
     hbm = pl.BlockSpec(memory_space=pltpu.HBM)
     smem = pl.BlockSpec(memory_space=pltpu.SMEM)
     f32 = jnp.float32
@@ -561,7 +574,7 @@
             jax.ShapeDtypeStruct((rows, dirs, bins, cols), f32),
             jax.ShapeDtypeStruct((rows, cols), f32),
         ),
-        in_specs=[smem] * 3 + [hbm] + [vmem] * 5,
+        in_specs=[smem] * 2 + [hbm] * 5,
         out_specs=(hbm, hbm),
         scratch_shapes=[
             pltpu.VMEM((rows, dirs, bins, cols), f32),
@@ -582,19 +595,23 @@
             pltpu.SemaphoreType.DMA((2, 3 * parts)),
             pltpu.SemaphoreType.DMA((2,)),
             pltpu.VMEM((rows, cols), f32),
+            pltpu.SMEM((2, dirs), f32),
+            pltpu.VMEM((rows, cols), f32),
+            pltpu.VMEM((rows, cols), jnp.int32),
+            pltpu.VMEM((rows, cols), jnp.int32),
+            pltpu.VMEM((rows, cols), f32),
+            pltpu.SemaphoreType.DMA((4,)),
             pltpu.SemaphoreType.DMA((rows, 2)),
             pltpu.SemaphoreType.DMA((4, parts)),
             pltpu.SemaphoreType.DMA(()),
         ],
         compiler_params=pltpu.CompilerParams(
-            collective_id=0, has_side_effects=True, vmem_limit_bytes=48 * 1024 * 1024
+            collective_id=0, has_side_effects=True, vmem_limit_bytes=63 * 1024 * 1024
         ),
     )(
         offsets,
         weights,
-        jnp.asarray(coefs),
         jnp.swapaxes(energy, 1, 2),
-        jnp.asarray(radian),
         water_depth,
         wet_mask,
         vegetation,

time: 59.6 us -> 52.2 us (0.88)
  local copies, waits for them, and re-layouts: 8.71 us -> 3.38 us
  Pallas kernels: 49.9 us -> 48 us
    unnamed x18 -> x4, local copies, waits for them, and re-layouts: 7.98 us -> 3.38 us
    pallas_call x1, Pallas kernels: 49.9 us -> 48 us  [kernel_body(): pl.pallas_call(functools.partial(kernel, groups, tiles, dirs), out_shape=...]
    another operation x1 -> x0, local copies, waits for them, and re-layouts: 0.73 us -> none
where the time goes in v4:
time: 52.2 us; the launch traced here: 52 us
  Pallas kernels  48 us (92%)
  local copies, waits for them, and re-layouts  3.38 us (6%)
  between operations  0.65 us (1%)
    pallas_call x1, Pallas kernels, kernel_body(): pl.pallas_call(functools.partial(kernel, groups, tiles, dirs), out_shape=...  48 us
    unnamed x4, local copies, waits for them, and re-layouts  3.38 us

profile of v4, /device:TPU:17, one launch (start us, length us, event | category | flops | bytes accessed | tf_op | source)
XLA Modules:
  0.0 52.0 jit_solution(9277189651282495428)
XLA Ops:
  0.6 48.0 %shard_map.86 = (f32[4,36,24,128]{3,2,1,0:T(8,128)}, f32[4,128]{1,0:T(4,128)}) custom-call(s32[4]{0:T(128)} %quad_offsets.1, f32[2]{0:T(128)} %quad_weights.1, f32[4,36,24,128]{3,2,1,0:T(8,128)} %bitcast.3, f32[4,128]{1,0:T(4,128)} %depth_in.1, s32[4,128]{1,0:T(4,128)} %wet_in.1, s32[4,128]{1,0:T(4,128)} %vegetation_in.1, f32[4,128]{1,0:T(4,128)} %canopy_in.1), custom_call_target="tpu_custom_call" | custom-call | tf_op jit(solution)/shard_map/pallas_call | solution.py:571
  48.6 0.0 copy-start
  48.6 2.8 %copy.11 = f32[4,24,36,128]{3,1,2,0:T(8,128)} copy(f32[4,24,36,128]{3,1,2,0:T(8,128)} %bitcast.2) | data formatting | bytes 3538944
  51.4 0.0 copy-done
  51.4 0.6 %copy.12 = f32[4,128]{1,0:T(4,128)} copy(f32[4,128]{1,0:T(4,128)S(1)} %copy-done) | data formatting | bytes 4096
Async XLA Ops:
  48.6 2.8 %copy-start = (f32[4,128]{1,0:T(4,128)S(1)}, f32[4,128]{1,0:T(4,128)}, u32[]{:S(2)}) copy-start(f32[4,128]{1,0:T(4,128)} %get-tuple-element.9) | copy-start | bytes 6148

commit v5 on v4

--- a/solution.py
+++ b/solution.py
@@ -165,6 +165,7 @@
 ROWS = 4
 REACH = 8
 PART = 3
+LAG = 2
 
 
 def sinh_of(x):
@@ -203,6 +204,7 @@
     incr,
     inbox,
     outbox,
+    relay,
     speed,
     wet,
     drag,
@@ -210,6 +212,7 @@
     part_theirs,
     send_sem,
     recv_sem,
+    relay_sems,
     fringe_sems,
     part_sems,
     orbit_row,
@@ -263,6 +266,16 @@
     def _():
         pl.semaphore_signal(barrier, inc=1, device_id=(mine, above_id), device_id_type=MESH)
 
+    planes = tiles // 4
+    place = lax.rem(tile, 4)
+    plane_here = lax.div(tile, 4)
+    friends = ((0, has_below, 2), (1, tile < tiles - 4, 3), (2, tile > 3, -3), (3, has_above, -2))
+    for at, active, offset in friends:
+
+        @pl.when(jnp.logical_and(place == at, active))
+        def _():
+            pl.semaphore_signal(barrier, inc=1, device_id=(mine, tile + offset), device_id_type=MESH)
+
     for j in range(dirs):
         angle = (j + 0.5) * 2.0 * math.pi / dirs
         coefs[0, j] = jnp.float32(abs(math.cos(angle)))
@@ -306,6 +319,85 @@
     empty = pl.multiple_of(mine * (REACH + bins), 8)
     leaving = pl.multiple_of(REACH + (1 - mine) * (bins - REACH), 8)
 
+    count = 2 * parts
+    crosses = {
+        True: jnp.logical_and(place == 3, has_above),
+        False: jnp.logical_and(place == 0, has_below),
+    }
+    crossing_plane = {True: plane_here, False: plane_here - 1}
+    relays = {
+        True: jnp.logical_and(place == 2, tile > 3),
+        False: jnp.logical_and(place == 1, tile < tiles - 4),
+    }
+    relay_plane = {True: plane_here - 1, False: plane_here}
+    to_relay = {True: 3, False: -3}
+    from_relay = {True: -2, False: 2}
+
+    def detours(plane, north, message):
+        share = plane + 1 if north else planes - 1 - plane
+        return lax.div((message + 1) * share, planes) > lax.div(message * share, planes)
+
+    def first_hop(step, n, north):
+        base = 0 if north else 2 * quarter
+        return pltpu.make_async_remote_copy(
+            src_ref=outbox.at[step, pl.ds(base + n * PART, PART)],
+            dst_ref=relay.at[step, pl.ds(n * PART, PART)],
+            send_sem=send_sem.at[step, (0 if north else 2) + lax.div(n, parts), lax.rem(n, parts)],
+            recv_sem=relay_sems.at[1, step, n],
+            device_id=(mine, tile + to_relay[north]),
+            device_id_type=MESH,
+        )
+
+    def second_hop(step, n, north):
+        base = 0 if north else 2 * quarter
+        return pltpu.make_async_remote_copy(
+            src_ref=relay.at[step, pl.ds(n * PART, PART)],
+            dst_ref=inbox.at[step, pl.ds(base + n * PART, PART)],
+            send_sem=relay_sems.at[0, step, n],
+            recv_sem=recv_sem.at[step, (0 if north else 2) + lax.div(n, parts), lax.rem(n, parts)],
+            device_id=(mine, tile + from_relay[north]),
+            device_id_type=MESH,
+        )
+
+    def send(step, q, k):
+        north = q < 2
+        n = (q % 2) * parts + k
+        around = jnp.logical_and(
+            crosses[north], detours(crossing_plane[north], north, step * count + n)
+        )
+
+        @pl.when(jnp.logical_and(sends(q), jnp.logical_not(around)))
+        def _():
+            edge(step, q, k).start()
+
+        @pl.when(around)
+        def _():
+            first_hop(step, n, north).start()
+
+    def forward(message):
+        step, n = lax.div(message, count), lax.rem(message, count)
+        for north in (True, False):
+
+            @pl.when(
+                jnp.logical_and(
+                    jnp.logical_and(relays[north], message < SUBSTEPS * count),
+                    detours(relay_plane[north], north, message),
+                )
+            )
+            def _():
+                first_hop(step, n, north).wait_recv()
+                second_hop(step, n, north).start()
+
+    def forward_sent(message):
+        step, n = lax.div(message, count), lax.rem(message, count)
+        for north in (True, False):
+
+            @pl.when(
+                jnp.logical_and(relays[north], detours(relay_plane[north], north, message))
+            )
+            def _():
+                second_hop(step, n, north).wait_send()
+
     def first_edges(k, carry):
         for q in (0, 2, 1, 3):
             row = ROWS - 1 if q < 2 else 0
@@ -313,15 +405,15 @@
                 j = q * quarter + k * PART + d
                 outbox[0, j] = speed[row] * (wet[row] * loaded[row, j])
 
-            @pl.when(sends(q))
-            def _():
-                edge(0, q, k).start()
+            send(0, q, k)
 
         return carry
 
     for row, side in urgent:
         load(row, side).wait()
     waits = 1 + has_below.astype(jnp.int32) + has_above.astype(jnp.int32)
+    for at, active, offset in friends:
+        waits = waits + jnp.logical_and(place == at, active).astype(jnp.int32)
     pl.semaphore_wait(barrier, waits)
     lax.fori_loop(0, parts, first_edges, 0)
     for row, side in later:
@@ -439,11 +531,9 @@
                     if last:
                         store(q, k).start()
                     else:
-
-                        @pl.when(sends(q))
-                        def _():
-                            edge(step + 1, q, k).start()
-
+                        send(step + 1, q, k)
+
+                forward(step * count + (near % 2) * parts + k + count - LAG)
                 if extra is not None:
                     extra((near % 2) * parts + k)
                 return carry
@@ -459,6 +549,11 @@
         substep(step, extra)
         return carry
 
+    def forward_first(message, carry):
+        forward(message)
+        return carry
+
+    lax.fori_loop(0, count - LAG, forward_first, 0)
     lax.fori_loop(0, 3, early_step, 0)
     substep(3)
 
@@ -552,6 +647,12 @@
         return lax.fori_loop(0, parts, piece, carry)
 
     lax.fori_loop(0, SUBSTEPS, drain, 0)
+
+    def drain_relay(message, carry):
+        forward_sent(message)
+        return carry
+
+    lax.fori_loop(0, SUBSTEPS * count, drain_relay, 0)
     orbit_copy.wait()
 
     def finish(k, carry):
@@ -562,9 +663,27 @@
     lax.fori_loop(0, parts, finish, 0)
 
 
+def hand_over(moved_in, orbital_in, moved, orbital, sems):
+    half = moved.shape[1] // 2
+    copies = [pltpu.make_async_copy(orbital_in, orbital, sems.at[2 * ROWS])]
+    for row in range(ROWS):
+        for side in range(2):
+            some = pl.ds(side * half, half)
+            copies.append(
+                pltpu.make_async_copy(
+                    moved_in.at[row, some], moved.at[row, some], sems.at[2 * row + side]
+                )
+            )
+    for copy in copies:
+        copy.start()
+    for copy in copies:
+        copy.wait()
+
+
 def kernel_body(groups, tiles, energy, water_depth, wet_mask, vegetation, canopy, offsets, weights):
     rows, bins, dirs, cols = energy.shape
     hbm = pl.BlockSpec(memory_space=pltpu.HBM)
+    anywhere = pl.BlockSpec(memory_space=pl.ANY)
     smem = pl.BlockSpec(memory_space=pltpu.SMEM)
     f32 = jnp.float32
     parts = dirs // 4 // PART
@@ -585,6 +704,7 @@
             pltpu.VMEM((dirs, rows, bins, cols), f32),
             pltpu.VMEM((SUBSTEPS, dirs, bins, cols), f32),
             pltpu.VMEM((SUBSTEPS, dirs, bins, cols), f32),
+            pltpu.VMEM((SUBSTEPS, dirs // 2, bins, cols), f32),
             pltpu.VMEM((rows, bins, cols), f32),
             pltpu.VMEM((rows, bins, cols), f32),
             pltpu.VMEM((rows, bins, cols), f32),
@@ -592,6 +712,7 @@
             pltpu.VMEM((rows, 8, cols), f32),
             pltpu.SemaphoreType.DMA((SUBSTEPS, 4, parts)),
             pltpu.SemaphoreType.DMA((SUBSTEPS, 4, parts)),
+            pltpu.SemaphoreType.DMA((2, SUBSTEPS, 2 * parts)),
             pltpu.SemaphoreType.DMA((2, 3 * parts)),
             pltpu.SemaphoreType.DMA((2,)),
             pltpu.VMEM((rows, cols), f32),
@@ -617,12 +738,23 @@
         vegetation,
         canopy,
     )
+    moved, orbital = pl.pallas_call(
+        hand_over,
+        out_shape=(
+            jax.ShapeDtypeStruct(moved.shape, f32),
+            jax.ShapeDtypeStruct(orbital.shape, f32),
+        ),
+        in_specs=[anywhere] * 2,
+        out_specs=(anywhere, anywhere),
+        scratch_shapes=[pltpu.SemaphoreType.DMA((2 * rows + 1,))],
+        compiler_params=pltpu.CompilerParams(vmem_limit_bytes=63 * 1024 * 1024),
+    )(moved, orbital)
     return jnp.swapaxes(moved, 1, 2), orbital
 
 
 def body(groups, tiles, energy, *rest):
     rows, bins, dirs, cols = energy.shape
-    if groups == 2 and rows == ROWS and bins % 8 == 0 and dirs % (4 * PART) == 0 and cols == 128:
+    if groups == 2 and rows == ROWS and bins % 8 == 0 and dirs % (4 * PART) == 0 and cols == 128 and tiles % 4 == 0:
         return kernel_body(groups, tiles, energy, *rest)
     return plain_body(energy, *rest)
 

time: 52.2 us -> 109 us (2.09)
  Pallas kernels: 48 us -> 107 us
  local copies, waits for them, and re-layouts: 3.38 us -> 0 us
    pallas_call x0 -> x1, Pallas kernels: none -> 54.9 us  [kernel_body(): pl.pallas_call(hand_over, out_shape=(jax.ShapeDtypeStruct(moved.shape, f3...]
    pallas_call x1, Pallas kernels: 48 us -> 52.5 us  [kernel_body(): pl.pallas_call(functools.partial(kernel, groups, tiles, dirs), out_shape=...]
    unnamed x4 -> x0, local copies, waits for them, and re-layouts: 3.38 us -> none
where the time goes in v5:
time: 109 us; the launch traced here: 108 us
  Pallas kernels  107 us (98%)
    pallas_call x1, Pallas kernels, kernel_body(): pl.pallas_call(hand_over, out_shape=(jax.ShapeDtypeStruct(moved.shape, f3...  54.9 us
    pallas_call x1, Pallas kernels, kernel_body(): pl.pallas_call(functools.partial(kernel, groups, tiles, dirs), out_shape=...  52.5 us

profile of v5, /device:TPU:17, one launch (start us, length us, event | category | flops | bytes accessed | tf_op | source)
XLA Modules:
  0.0 108.0 jit_solution(17315741716244369210)
XLA Ops:
  0.6 52.5 %shard_map.86 = (f32[4,36,24,128]{3,2,1,0:T(8,128)}, f32[4,128]{1,0:T(4,128)}) custom-call(s32[4]{0:T(128)} %quad_offsets.1, f32[2]{0:T(128)} %quad_weights.1, f32[4,36,24,128]{3,2,1,0:T(8,128)} %bitcast.2, f32[4,128]{1,0:T(4,128)} %depth_in.1, s32[4,128]{1,0:T(4,128)} %wet_in.1, s32[4,128]{1,0:T(4,128)} %vegetation_in.1, f32[4,128]{1,0:T(4,128)} %canopy_in.1), custom_call_target="tpu_custom_call" | custom-call | tf_op jit(solution)/shard_map/pallas_call | solution.py:690
  53.2 54.9 %shard_map.87 = (f32[4,36,24,128]{3,2,1,0:T(8,128)}, f32[4,128]{1,0:T(4,128)}) custom-call(f32[4,36,24,128]{3,2,1,0:T(8,128)} %get-tuple-element.6.moved_in, f32[4,128]{1,0:T(4,128)} %get-tuple-element.7.orbital_in), custom_call_target="tpu_custom_call" | custom-call | tf_op jit(solution)/shard_map/pallas_call | solution.py:741

commit v6 on v4

--- a/solution.py
+++ b/solution.py
@@ -164,7 +164,7 @@
 MESH = pl.DeviceIdType.MESH
 ROWS = 4
 REACH = 8
-PART = 3
+PART = 9
 
 
 def sinh_of(x):
@@ -560,6 +560,11 @@
         return carry
 
     lax.fori_loop(0, parts, finish, 0)
+
+
+def hand_over(moved_in, orbital_in, moved, orbital):
+    moved[...] = moved_in[...]
+    orbital[...] = orbital_in[...]
 
 
 def kernel_body(groups, tiles, energy, water_depth, wet_mask, vegetation, canopy, offsets, weights):
@@ -617,6 +622,19 @@
         vegetation,
         canopy,
     )
+    block = pl.BlockSpec((1, dirs // 2, bins, cols), lambda i: (i // 2, i % 2, 0, 0))
+    whole = pl.BlockSpec((rows, cols), lambda i: (0, 0))
+    moved, orbital = pl.pallas_call(
+        hand_over,
+        grid=(2 * rows,),
+        out_shape=(
+            jax.ShapeDtypeStruct(moved.shape, f32),
+            jax.ShapeDtypeStruct(orbital.shape, f32),
+        ),
+        in_specs=[block, whole],
+        out_specs=(block, whole),
+        compiler_params=pltpu.CompilerParams(vmem_limit_bytes=63 * 1024 * 1024),
+    )(moved, orbital)
     return jnp.swapaxes(moved, 1, 2), orbital
 
 

time: 52.2 us -> 53.7 us (1.029)
  the two profiles are of different devices: /device:TPU:17 before, /device:TPU:19 now
where the time goes in v6:
time: 53.7 us; the launch traced here: 53.4 us
  Pallas kernels  52.8 us (98%)
  between operations  0.64 us (1%)
    pallas_call x1, Pallas kernels, kernel_body(): pl.pallas_call(functools.partial(kernel, groups, tiles, dirs), out_shape=...  47.2 us
    pallas_call x1, Pallas kernels, kernel_body(): pl.pallas_call(hand_over, grid=(2 * rows,), out_shape=(jax.ShapeDtypeStru...  5.56 us

profile of v6, /device:TPU:19, one launch (start us, length us, event | category | flops | bytes accessed | tf_op | source)
XLA Modules:
  0.0 53.4 jit_solution(7495056560016879342)
XLA Ops:
  0.6 47.2 %shard_map.86 = (f32[4,36,24,128]{3,2,1,0:T(8,128)}, f32[4,128]{1,0:T(4,128)}) custom-call(s32[4]{0:T(128)} %quad_offsets.1, f32[2]{0:T(128)} %quad_weights.1, f32[4,36,24,128]{3,2,1,0:T(8,128)} %bitcast.2, f32[4,128]{1,0:T(4,128)} %depth_in.1, s32[4,128]{1,0:T(4,128)} %wet_in.1, s32[4,128]{1,0:T(4,128)} %vegetation_in.1, f32[4,128]{1,0:T(4,128)} %canopy_in.1), custom_call_target="tpu_custom_call" | custom-call | tf_op jit(solution)/shard_map/pallas_call | solution.py:576
  47.8 5.6 %shard_map.87 = (f32[4,36,24,128]{3,2,1,0:T(8,128)}, f32[4,128]{1,0:T(4,128)}) custom-call(f32[4,36,24,128]{3,2,1,0:T(8,128)} %get-tuple-element.6.moved_in, f32[4,128]{1,0:T(4,128)} %get-tuple-element.7.orbital_in), custom_call_target="tpu_custom_call" | custom-call | tf_op jit(solution)/shard_map/pallas_call | solution.py:627

commit v7 on v1

--- a/solution.py
+++ b/solution.py
@@ -165,7 +165,7 @@
 MESH = pl.DeviceIdType.MESH
 ROWS = 4
 REACH = 8
-PART = 3
+PART = 9
 
 
 def sinh_of(x):

time: 51.1 us -> 49.8 us (0.975)
  Pallas kernels: 46.4 us -> 45.2 us
    pallas_call x1, Pallas kernels: 46.4 us -> 45.2 us  [kernel_body(): pl.pallas_call(functools.partial(kernel, groups, tiles, dirs), out_shape=...]
where the time goes in v7:
time: 49.8 us; the launch traced here: 49.7 us
  Pallas kernels  45.2 us (91%)
  local copies, waits for them, and re-layouts  3.75 us (8%)
  between operations  0.76 us (2%)
    pallas_call x1, Pallas kernels, kernel_body(): pl.pallas_call(functools.partial(kernel, groups, tiles, dirs), out_shape=...  45.2 us
    unnamed x19, local copies, waits for them, and re-layouts  3.68 us

profile of v7, /device:TPU:17, one launch (start us, length us, event | category | flops | bytes accessed | tf_op | source)
XLA Modules:
  0.0 49.7 jit_solution(10875388945762124481)
XLA Ops:
  0.6 0.0 copy-start.7
  0.6 0.0 copy-start.4
  0.7 0.0 copy-start.6
  0.7 0.0 copy-start.5
  0.7 0.0 copy-start.3
  0.7 0.0 copy-start.2
  0.7 0.0 copy-start.1
  0.7 0.0 copy-start
  0.7 1.7 %copy.14 = f32[4,24,36,128]{3,1,0,2:T(8,128)S(1)} copy(f32[4,24,36,128]{3,1,2,0:T(8,128)} %param.9) | data formatting | bytes 3538944 | tf_op args[0]
  2.5 0.0 copy-done.7
  2.5 0.1 jit_solution_.3.radian
  2.5 0.0 copy-done.4
  2.5 0.0 copy-done.6
  2.5 0.0 copy-done.5
  2.6 0.0 copy-done.3
  2.6 0.0 copy-done.2
  2.6 0.0 copy-done.1
  2.6 0.0 copy-done
  2.6 45.2 %shard_map.104 = (f32[36,4,24,128]{3,2,1,0:T(8,128)S(1)}, f32[4,128]{1,0:T(4,128)S(1)}) custom-call(s32[4]{0:T(128)S(1)} %copy-done.5, f32[2]{0:T(128)S(1)} %copy-done.6, f32[2,36]{1,0:T(2,128)S(1)} %copy-done.4, f32[36,4,24,128]{3,2,1,0:T(8,128)S(1)} %bitcast.4, f32[48,128]{1,0:T(8,128)S(1)} %jit_solution_.3.radian, f32[4,128]{1,0:T(4,128)S(1)} %copy-done, ...), custom_call_target="tpu_custom_call" | custom-call | tf_op jit(solution)/shard_map/pallas_call | solution.py:504
  47.8 1.3 %copy.12 = f32[4,24,36,128]{3,1,2,0:T(8,128)} copy(f32[4,24,36,128]{3,1,0,2:T(8,128)S(1)} %bitcast.5) | data formatting | bytes 3538944
  49.1 0.6 %copy.16 = f32[4,128]{1,0:T(4,128)} copy(f32[4,128]{1,0:T(4,128)S(1)} %get-tuple-element.11) | data formatting | bytes 4096
Async XLA Ops:
  0.6 1.8 %copy-start.7 = (f32[48]{0:T(128)S(1)}, f32[48]{0:T(128)}, u32[]{:S(2)}) copy-start(f32[48]{0:T(128)} %constant.5.clone) | copy-start | bytes 580
  0.6 1.9 %copy-start.4 = (f32[2,36]{1,0:T(2,128)S(1)}, f32[2,36]{1,0:T(2,128)}, u32[]{:S(2)}) copy-start(f32[2,36]{1,0:T(2,128)} %constant.4.clone.coefs) | copy-start | bytes 868
  0.7 1.9 %copy-start.6 = (f32[2]{0:T(128)S(1)}, f32[2]{0:T(128)}, u32[]{:S(2)}) copy-start(f32[2]{0:T(128)} %quad_weights.1) | copy-start | bytes 28
  0.7 1.9 %copy-start.5 = (s32[4]{0:T(128)S(1)}, s32[4]{0:T(128)}, u32[]{:S(2)}) copy-start(s32[4]{0:T(128)} %quad_offsets.1) | copy-start | bytes 52
  0.7 1.9 %copy-start.3 = (f32[4,128]{1,0:T(4,128)S(1)}, f32[4,128]{1,0:T(4,128)}, u32[]{:S(2)}) copy-start(f32[4,128]{1,0:T(4,128)} %canopy.1) | copy-start | bytes 6148
  0.7 1.9 %copy-start.2 = (s32[4,128]{1,0:T(4,128)S(1)}, s32[4,128]{1,0:T(4,128)}, u32[]{:S(2)}) copy-start(s32[4,128]{1,0:T(4,128)} %vegetation.1) | copy-start | bytes 6148
  0.7 1.9 %copy-start.1 = (s32[4,128]{1,0:T(4,128)S(1)}, s32[4,128]{1,0:T(4,128)}, u32[]{:S(2)}) copy-start(s32[4,128]{1,0:T(4,128)} %wet_mask.1) | copy-start | bytes 6148
  0.7 1.9 %copy-start = (f32[4,128]{1,0:T(4,128)S(1)}, f32[4,128]{1,0:T(4,128)}, u32[]{:S(2)}) copy-start(f32[4,128]{1,0:T(4,128)} %depth.1) | copy-start | bytes 6148
